TPU v7x, 512 devices: a whole 4x8x8 slice. The times are simulated.
512 devices in a mesh: gx: 32 (over y_hi, z, core), gz: 16 (over x, y_lo).
Axes of the slice: x: 4, y: 8 (y_hi: 2, y_lo: 4; y = y_hi * 4 + y_lo), z: 8, core: 2. Of those that a mesh axis runs over, the one named last changes fastest.
Arguments:
- u_field: float32 [2, 8192, 2048], P(None, 'gx', 'gz'), may hold values from -6 to 6
- w_field: float32 [2, 8192, 2048], P(None, 'gx', 'gz'), may hold values from -6 to 6
- temp_field: float32 [2, 8192, 2048], P(None, 'gx', 'gz'), may hold values from -6 to 6
Outputs:
- temp_tendency: float32 [2, 8192, 2048], P(None, 'gx', 'gz')
All inputs are finite; a program needn't handle non-finite values.
Results may differ from a plain program's by a relative error of at most 0.00012.
Values sent between devices are 32-bit elements; how exact they have to be, the bound alone decides.
A program may use at most 128 MiB of HBM per device.

v0:
```python
import math

import jax
import jax.numpy as jnp
from jax import lax
from jax.sharding import PartitionSpec as P

full_turn = 2.0 * math.pi
conduction_coefficient = 0.3
highest = lax.Precision.HIGHEST


def partner_2(value, axis, bit):
    return lax.ppermute(value, axis, [(i, i ^ 1 << bit) for i in range(lax.axis_size(axis))])


def extended(value, sides, width):
    for axis, dim in sides:
        peers, length = (lax.axis_size(axis), value.shape[dim])
        up = [(i, (i + 1) % peers) for i in range(peers - 1)]
        down = [(j, i) for i, j in up]
        last = lax.slice_in_dim(value, length - width, length, axis=dim)
        first = lax.slice_in_dim(value, 0, width, axis=dim)
        before = lax.ppermute(last, axis, up)
        after = lax.ppermute(first, axis, down)
        value = jnp.concatenate([before, value, after], axis=dim)
    return value


def complex_times(values, cosine_part, sine_part):
    real_part = values[0] * cosine_part - values[1] * sine_part
    imag_part = values[0] * sine_part + values[1] * cosine_part
    return jnp.stack([real_part, imag_part])


def fourier_matrix(length, direction, factor):
    integers = jnp.arange(length, dtype=jnp.int32)
    exponent = integers[:, None] * integers[None, :] % length
    phase_angle = direction * full_turn * exponent.astype(jnp.float32) / length
    cosine_part = jnp.cos(phase_angle) * factor
    sine_part = jnp.sin(phase_angle) * factor
    upper_rows = jnp.concatenate([cosine_part, -sine_part], axis=1)
    lower_rows = jnp.concatenate([sine_part, cosine_part], axis=1)
    return jnp.concatenate([upper_rows, lower_rows], axis=0).reshape(2, length, 2, length)


def apply_matrix(matrix, values):
    return jnp.einsum("akbm,bfymz->afykz", matrix, values, precision=highest)


def pair_twiddle(section_bit, local_len, device_index, direction):
    low_bits = device_index & (1 << section_bit) - 1
    offset = low_bits * local_len + jnp.arange(local_len, dtype=jnp.int32)
    subproblem = (1 << section_bit + 1) * local_len
    phase_angle = direction * full_turn * offset.astype(jnp.float32) / subproblem
    high_bit = device_index >> section_bit & 1
    cosine_part = jnp.where(high_bit == 1, jnp.cos(phase_angle), 1.0)[:, None]
    sine_part = jnp.where(high_bit == 1, jnp.sin(phase_angle), 0.0)[:, None]
    return (high_bit, cosine_part, sine_part)


def butterfly_forward(values, paired):
    section_count = lax.axis_size("gx").bit_length() - 1
    device_index = lax.axis_index("gx")
    local_len = values.shape[3]
    for section_bit in range(section_count - 1, -1, -1):
        if paired:
            partner = partner_2(values, "gx", section_bit)
        else:
            partner = partner_2(values, "gx", section_bit)
        high_bit, cosine_part, sine_part = pair_twiddle(section_bit, local_len, device_index, -1.0)
        signed_own = (1 - 2 * high_bit).astype(jnp.float32)
        values = complex_times(partner + signed_own * values, cosine_part, sine_part)
    return apply_matrix(fourier_matrix(local_len, -1.0, 1.0), values)


def butterfly_inverse(values, paired):
    section_count = lax.axis_size("gx").bit_length() - 1
    device_index = lax.axis_index("gx")
    local_len = values.shape[3]
    values = apply_matrix(fourier_matrix(local_len, 1.0, 1.0 / local_len), values)
    for section_bit in range(section_count):
        high_bit, cosine_part, sine_part = pair_twiddle(section_bit, local_len, device_index, 1.0)
        outgoing = complex_times(values, cosine_part, sine_part)
        if paired:
            partner = partner_2(outgoing, "gx", section_bit)
        else:
            partner = partner_2(outgoing, "gx", section_bit)
        signed_own = (1 - 2 * high_bit).astype(jnp.float32)
        values = 0.5 * (partner + signed_own * outgoing)
    return values


def forward_along(values, paired):
    return butterfly_forward(values, paired)


def inverse_along(values, paired):
    return butterfly_inverse(values, paired)


def spectral_terms(mode_index, total_len):
    signed = jnp.where(mode_index < total_len // 2, mode_index, mode_index - total_len)
    kept_modes = (3 * jnp.abs(signed) <= total_len).astype(jnp.float32)[:, None]
    wavenumber = (full_turn * signed.astype(jnp.float32) / total_len)[:, None]
    return (kept_modes, wavenumber)


def shards(u_field, w_field, temp_field):
    axis_len = lax.axis_size("gx")
    section_count = axis_len.bit_length() - 1
    device_index = lax.axis_index("gx")
    local_len = u_field.shape[1]
    total_len = axis_len * local_len
    zero_field = jnp.zeros_like(temp_field)
    packed = jnp.stack([jnp.stack([u_field, temp_field]), jnp.stack([w_field, zero_field])])
    spectra = forward_along(packed, True)
    first_mode = jnp.zeros((), jnp.int32)
    for section_bit in range(section_count):
        first_mode = first_mode + (
            (device_index >> section_bit & 1) << section_count - 1 - section_bit
        )
    mode_index = first_mode + axis_len * jnp.arange(local_len, dtype=jnp.int32)
    kept_modes, wavenumber = spectral_terms(mode_index, total_len)
    filtered = spectra * kept_modes
    point_value_domain = inverse_along(filtered, True)
    lateral_wind_speed = point_value_domain[0, 0]
    upward_wind_speed = point_value_domain[1, 0]
    current_warmth_profile = point_value_domain[0, 1]
    warmth_transport_samples = lateral_wind_speed * current_warmth_profile
    warmth_transport_modes = forward_along(
        jnp.stack([warmth_transport_samples, zero_field])[:, None], False
    )
    temp_spec = filtered[:, 1]
    damping = conduction_coefficient * wavenumber * wavenumber
    tendency_real = wavenumber * warmth_transport_modes[1, 0] - damping * temp_spec[0]
    tendency_imag = -wavenumber * warmth_transport_modes[0, 0] - damping * temp_spec[1]
    horizontal = inverse_along(jnp.stack([tendency_real, tendency_imag])[:, None], False)[0, 0]
    joined_quantity_arrays = jnp.stack(
        [upward_wind_speed * current_warmth_profile, current_warmth_profile]
    )
    enlarged_sample_points = extended(joined_quantity_arrays, (("gz", 3),), 1)
    upward_levels_count = -0.5 * (
        enlarged_sample_points[0, :, :, 2:] - enlarged_sample_points[0, :, :, :-2]
    )
    upward_levels_count = upward_levels_count + conduction_coefficient * (
        enlarged_sample_points[1, :, :, 2:]
        - 2.0 * current_warmth_profile
        + enlarged_sample_points[1, :, :, :-2]
    )
    return horizontal + upward_levels_count


def solution(mesh):
    in_specs = (P(None, "gx", "gz"), P(None, "gx", "gz"), P(None, "gx", "gz"))
    out_specs = P(None, "gx", "gz")
    return jax.shard_map(shards, mesh=mesh, in_specs=in_specs, out_specs=out_specs, check_vma=False)
```

profile of v0, /device:TPU:1, one launch (start us, length us, event | category | flops | bytes accessed | tf_op | source)
XLA Modules:
  0.0 584.9 jit_solution(16246157704178002405)
XLA Ops:
  2.4 8.3 %collective-permute-start = (f32[2,2,2,256,128]{3,4,0,2,1:T(8,128)S(1)}, f32[2,2,2,256,128]{3,4,0,2,1:T(8,128)S(1)}, u32[]{:S(2)}, u32[]{:S(2)}) collective-permute-start(f32[2,2,2,256,128]{3,4,0,2,1:T(8,128)S(1)} %pad_maximum_fusion), channel_id=1, source_target_pairs={{0,256},{16,272},{32,288},{48,304},{64,320},{80,336},{96,352},{112... | collective-permute-start | bytes 3145736 | tf_op jit(solution)/shard_map/ppermute | solution.py:14
  10.7 33.9 %collective-permute-done = f32[2,2,2,256,128]{3,4,0,2,1:T(8,128)S(1)} collective-permute-done((f32[2,2,2,256,128]{3,4,0,2,1:T(8,128)S(1)}, f32[2,2,2,256,128]{3,4,0,2,1:T(8,128)S(1)}, u32[]{:S(2)}, u32[]{:S(2)}) %collective-permute-start) | collective-permute-done | bytes 1048608 | tf_op jit(solution)/shard_map/ppermute | solution.py:14
  45.0 11.2 %collective-permute-start.1 = (f32[2,2,2,256,128]{3,4,0,2,1:T(8,128)S(1)}, f32[2,2,2,256,128]{3,4,0,2,1:T(8,128)S(1)}, u32[]{:S(2)}, u32[]{:S(2)}) collective-permute-start(f32[2,2,2,256,128]{3,4,0,2,1:T(8,128)S(1)} %pad_maximum_fusion.1), channel_id=1, source_target_pairs={{0,128},{16,144},{32,160},{48,176},{64,192},{80,208},{96,224},{112... | collective-permute-start | bytes 3145736 | tf_op jit(solution)/shard_map/ppermute | solution.py:14
  56.2 12.3 %collective-permute-done.1 = f32[2,2,2,256,128]{3,4,0,2,1:T(8,128)S(1)} collective-permute-done((f32[2,2,2,256,128]{3,4,0,2,1:T(8,128)S(1)}, f32[2,2,2,256,128]{3,4,0,2,1:T(8,128)S(1)}, u32[]{:S(2)}, u32[]{:S(2)}) %collective-permute-start.1) | collective-permute-done | bytes 1048608 | tf_op jit(solution)/shard_map/ppermute | solution.py:14
  68.9 37.2 %collective-permute-start.2 = (f32[2,2,2,256,128]{3,4,0,2,1:T(8,128)S(1)}, f32[2,2,2,256,128]{3,4,0,2,1:T(8,128)S(1)}, u32[]{:S(2)}, u32[]{:S(2)}) collective-permute-start(f32[2,2,2,256,128]{3,4,0,2,1:T(8,128)S(1)} %pad_maximum_fusion.2), channel_id=1, source_target_pairs={{0,64},{16,80},{32,96},{48,112},{64,0},{80,16},{96,32},{112,48},{1... | collective-permute-start | bytes 3145736 | tf_op jit(solution)/shard_map/ppermute | solution.py:14
  106.2 42.4 %collective-permute-done.2 = f32[2,2,2,256,128]{3,4,0,2,1:T(8,128)S(1)} collective-permute-done((f32[2,2,2,256,128]{3,4,0,2,1:T(8,128)S(1)}, f32[2,2,2,256,128]{3,4,0,2,1:T(8,128)S(1)}, u32[]{:S(2)}, u32[]{:S(2)}) %collective-permute-start.2) | collective-permute-done | bytes 1048608 | tf_op jit(solution)/shard_map/ppermute | solution.py:14
  151.0 24.1 %collective-permute-done.3 = f32[2,2,2,256,128]{3,4,0,2,1:T(8,128)S(1)} collective-permute-done((f32[2,2,2,256,128]{3,4,0,2,1:T(8,128)S(1)}, f32[2,2,2,256,128]{3,4,0,2,1:T(8,128)S(1)}, u32[]{:S(2)}, u32[]{:S(2)}) %collective-permute-start.3) | collective-permute-done | bytes 1048608 | tf_op jit(solution)/shard_map/ppermute | solution.py:14
  176.5 3.4 collective-permute-start.4
  193.4 1.9 collective-permute-start.5
  195.4 2.6 collective-permute-done.5
  200.3 24.5 %collective-permute-done.6 = f32[2,2,2,256,128]{3,4,0,2,1:T(8,128)S(1)} collective-permute-done((f32[2,2,2,256,128]{3,4,0,2,1:T(8,128)S(1)}, f32[2,2,2,256,128]{3,4,0,2,1:T(8,128)S(1)}, u32[]{:S(2)}, u32[]{:S(2)}) %collective-permute-start.6) | collective-permute-done | bytes 1048608 | tf_op jit(solution)/shard_map/ppermute | solution.py:14
  227.2 48.1 %collective-permute-done.7 = f32[2,2,2,256,128]{3,4,0,2,1:T(8,128)S(1)} collective-permute-done((f32[2,2,2,256,128]{3,4,0,2,1:T(8,128)S(1)}, f32[2,2,2,256,128]{3,4,0,2,1:T(8,128)S(1)}, u32[]{:S(2)}, u32[]{:S(2)}) %collective-permute-start.7) | collective-permute-done | bytes 1048608 | tf_op jit(solution)/shard_map/ppermute | solution.py:14
  275.7 7.1 %collective-permute-start.8 = (f32[2,2,2,256,128]{3,4,0,2,1:T(8,128)S(1)}, f32[2,2,2,256,128]{3,4,0,2,1:T(8,128)S(1)}, u32[]{:S(2)}, u32[]{:S(2)}) collective-permute-start(f32[2,2,2,256,128]{3,4,0,2,1:T(8,128)S(1)} %pad_maximum_fusion.8), channel_id=1, source_target_pairs={{0,128},{16,144},{32,160},{48,176},{64,192},{80,208},{96,224},{112... | collective-permute-start | bytes 3145736 | tf_op jit(solution)/shard_map/ppermute | solution.py:14
  282.8 45.5 %collective-permute-done.8 = f32[2,2,2,256,128]{3,4,0,2,1:T(8,128)S(1)} collective-permute-done((f32[2,2,2,256,128]{3,4,0,2,1:T(8,128)S(1)}, f32[2,2,2,256,128]{3,4,0,2,1:T(8,128)S(1)}, u32[]{:S(2)}, u32[]{:S(2)}) %collective-permute-start.8) | collective-permute-done | bytes 1048608 | tf_op jit(solution)/shard_map/ppermute | solution.py:14
  328.7 7.4 %collective-permute-start.9 = (f32[2,2,2,256,128]{3,4,0,2,1:T(8,128)S(1)}, f32[2,2,2,256,128]{3,4,0,2,1:T(8,128)S(1)}, u32[]{:S(2)}, u32[]{:S(2)}) collective-permute-start(f32[2,2,2,256,128]{3,4,0,2,1:T(8,128)S(1)} %pad_maximum_fusion.9), channel_id=1, source_target_pairs={{0,256},{16,272},{32,288},{48,304},{64,320},{80,336},{96,352},{112... | collective-permute-start | bytes 3145736 | tf_op jit(solution)/shard_map/ppermute | solution.py:14
  336.2 22.1 %collective-permute-done.9 = f32[2,2,2,256,128]{3,4,0,2,1:T(8,128)S(1)} collective-permute-done((f32[2,2,2,256,128]{3,4,0,2,1:T(8,128)S(1)}, f32[2,2,2,256,128]{3,4,0,2,1:T(8,128)S(1)}, u32[]{:S(2)}, u32[]{:S(2)}) %collective-permute-start.9) | collective-permute-done | bytes 1048608 | tf_op jit(solution)/shard_map/ppermute | solution.py:14
  358.5 7.2 %collective-permute-start.10 = (f32[2,1,2,256,128]{3,4,2,0,1:T(8,128)S(1)}, f32[2,1,2,256,128]{3,4,2,0,1:T(8,128)S(1)}, u32[]{:S(2)}, u32[]{:S(2)}) collective-permute-start(f32[2,1,2,256,128]{3,4,2,0,1:T(8,128)S(1)} %pad_bitcast_fusion), channel_id=1, source_target_pairs={{0,256},{16,272},{32,288},{48,304},{64,320},{80,336},{96,352},{112... | collective-permute-start | bytes 1572872 | tf_op jit(solution)/shard_map/ppermute | solution.py:14
  365.7 28.2 %collective-permute-done.10 = f32[2,1,2,256,128]{3,4,2,0,1:T(8,128)S(1)} collective-permute-done((f32[2,1,2,256,128]{3,4,2,0,1:T(8,128)S(1)}, f32[2,1,2,256,128]{3,4,2,0,1:T(8,128)S(1)}, u32[]{:S(2)}, u32[]{:S(2)}) %collective-permute-start.10) | collective-permute-done | bytes 524320 | tf_op jit(solution)/shard_map/ppermute | solution.py:14
  394.0 4.5 collective-permute-start.11
  398.5 16.7 %collective-permute-done.11 = f32[2,1,2,256,128]{3,4,2,1,0:T(8,128)S(1)} collective-permute-done((f32[2,1,2,256,128]{3,4,2,1,0:T(8,128)S(1)}, f32[2,1,2,256,128]{3,4,2,1,0:T(8,128)S(1)}, u32[]{:S(2)}, u32[]{:S(2)}) %collective-permute-start.11) | collective-permute-done | bytes 524320 | tf_op jit(solution)/shard_map/ppermute | solution.py:14
  417.3 20.5 %collective-permute-done.12 = f32[2,1,2,256,128]{3,4,2,1,0:T(8,128)S(1)} collective-permute-done((f32[2,1,2,256,128]{3,4,2,1,0:T(8,128)S(1)}, f32[2,1,2,256,128]{3,4,2,1,0:T(8,128)S(1)}, u32[]{:S(2)}, u32[]{:S(2)}) %collective-permute-start.12) | collective-permute-done | bytes 524320 | tf_op jit(solution)/shard_map/ppermute | solution.py:14
  439.9 13.0 %collective-permute-done.13 = f32[2,1,2,256,128]{3,4,2,1,0:T(8,128)S(1)} collective-permute-done((f32[2,1,2,256,128]{3,4,2,1,0:T(8,128)S(1)}, f32[2,1,2,256,128]{3,4,2,1,0:T(8,128)S(1)}, u32[]{:S(2)}, u32[]{:S(2)}) %collective-permute-start.13) | collective-permute-done | bytes 524320 | tf_op jit(solution)/shard_map/ppermute | solution.py:14
  453.1 3.2 collective-permute-start.14
  460.3 2.3 collective-permute-start.15
  464.3 1.9 collective-permute-start.16
  466.3 13.1 %collective-permute-done.16 = f32[2,1,2,256,128]{3,4,2,1,0:T(8,128)S(1)} collective-permute-done((f32[2,1,2,256,128]{3,4,2,1,0:T(8,128)S(1)}, f32[2,1,2,256,128]{3,4,2,1,0:T(8,128)S(1)}, u32[]{:S(2)}, u32[]{:S(2)}) %collective-permute-start.16) | collective-permute-done | bytes 524320 | tf_op jit(solution)/shard_map/ppermute | solution.py:14
  481.5 25.7 %collective-permute-done.17 = f32[2,1,2,256,128]{3,4,2,1,0:T(8,128)S(1)} collective-permute-done((f32[2,1,2,256,128]{3,4,2,1,0:T(8,128)S(1)}, f32[2,1,2,256,128]{3,4,2,1,0:T(8,128)S(1)}, u32[]{:S(2)}, u32[]{:S(2)}) %collective-permute-start.17) | collective-permute-done | bytes 524320 | tf_op jit(solution)/shard_map/ppermute | solution.py:14
  507.3 2.5 collective-permute-start.18
  509.9 25.5 %collective-permute-done.18 = f32[2,1,2,256,128]{3,4,2,1,0:T(8,128)S(1)} collective-permute-done((f32[2,1,2,256,128]{3,4,2,1,0:T(8,128)S(1)}, f32[2,1,2,256,128]{3,4,2,1,0:T(8,128)S(1)}, u32[]{:S(2)}, u32[]{:S(2)}) %collective-permute-start.18) | collective-permute-done | bytes 524320 | tf_op jit(solution)/shard_map/ppermute | solution.py:14
  535.6 2.7 collective-permute-start.19
  539.6 37.9 %collective-permute-start.21 = (f32[2,2,256,1]{2,3,1,0:T(1,128)S(1)}, f32[2,2,256,1]{2,3,1,0:T(1,128)S(1)}, u32[]{:S(2)}, u32[]{:S(2)}) collective-permute-start(f32[2,2,256,1]{2,3,1,0:T(1,128)S(1)} %get-tuple-element.50), channel_id=1, source_target_pairs={{0,1},{1,2},{2,3},{3,4},{4,5},{5,6},{6,7},{7,8},{8,9},{9,10},{10,1... | collective-permute-start | bytes 12296 | tf_op jit(solution)/shard_map/ppermute | solution.py:24
  577.5 6.4 %collective-permute-done.20 = f32[2,2,256,1]{2,3,1,0:T(1,128)S(1)} collective-permute-done((f32[2,2,256,1]{2,3,1,0:T(1,128)S(1)}, f32[2,2,256,1]{2,3,1,0:T(1,128)S(1)}, u32[]{:S(2)}, u32[]{:S(2)}) %collective-permute-start.20) | collective-permute-done | bytes 4128 | tf_op jit(solution)/shard_map/ppermute | solution.py:25
  (110 shorter events, 40.7 us)
Async XLA Ops:
  0.0 1.1 copy-start
  1.1 1.0 copy-start.1
  2.4 42.2 %collective-permute-start = (f32[2,2,2,256,128]{3,4,0,2,1:T(8,128)S(1)}, f32[2,2,2,256,128]{3,4,0,2,1:T(8,128)S(1)}, u32[]{:S(2)}, u32[]{:S(2)}) collective-permute-start(f32[2,2,2,256,128]{3,4,0,2,1:T(8,128)S(1)} %pad_maximum_fusion), channel_id=1, source_target_pairs={{0,256},{16,272},{32,288},{48,304},{64,320},{80,336},{96,352},{112... | collective-permute-start | bytes 3145736 | tf_op jit(solution)/shard_map/ppermute | solution.py:14
  45.0 23.6 %collective-permute-start.1 = (f32[2,2,2,256,128]{3,4,0,2,1:T(8,128)S(1)}, f32[2,2,2,256,128]{3,4,0,2,1:T(8,128)S(1)}, u32[]{:S(2)}, u32[]{:S(2)}) collective-permute-start(f32[2,2,2,256,128]{3,4,0,2,1:T(8,128)S(1)} %pad_maximum_fusion.1), channel_id=1, source_target_pairs={{0,128},{16,144},{32,160},{48,176},{64,192},{80,208},{96,224},{112... | collective-permute-start | bytes 3145736 | tf_op jit(solution)/shard_map/ppermute | solution.py:14
  68.9 79.7 %collective-permute-start.2 = (f32[2,2,2,256,128]{3,4,0,2,1:T(8,128)S(1)}, f32[2,2,2,256,128]{3,4,0,2,1:T(8,128)S(1)}, u32[]{:S(2)}, u32[]{:S(2)}) collective-permute-start(f32[2,2,2,256,128]{3,4,0,2,1:T(8,128)S(1)} %pad_maximum_fusion.2), channel_id=1, source_target_pairs={{0,64},{16,80},{32,96},{48,112},{64,0},{80,16},{96,32},{112,48},{1... | collective-permute-start | bytes 3145736 | tf_op jit(solution)/shard_map/ppermute | solution.py:14
  149.0 26.1 %collective-permute-start.3 = (f32[2,2,2,256,128]{3,4,0,2,1:T(8,128)S(1)}, f32[2,2,2,256,128]{3,4,0,2,1:T(8,128)S(1)}, u32[]{:S(2)}, u32[]{:S(2)}) collective-permute-start(f32[2,2,2,256,128]{3,4,0,2,1:T(8,128)S(1)} %pad_maximum_fusion.3), channel_id=1, source_target_pairs={{0,32},{16,48},{32,0},{48,16},{64,96},{80,112},{96,64},{112,80},{1... | collective-permute-start | bytes 3145736 | tf_op jit(solution)/shard_map/ppermute | solution.py:14
  176.5 11.4 %collective-permute-start.4 = (f32[2,2,2,256,128]{3,4,0,2,1:T(8,128)}, f32[2,2,2,256,128]{3,4,0,2,1:T(8,128)}, u32[]{:S(2)}, u32[]{:S(2)}) collective-permute-start(f32[2,2,2,256,128]{3,4,0,2,1:T(8,128)} %pad_maximum_fusion.4), channel_id=1, source_target_pairs={{0,16},{16,0},{32,48},{48,32},{64,80},{80,64},{96,112},{112,96},{1... | collective-permute-start | bytes 3145736 | tf_op jit(solution)/shard_map/ppermute | solution.py:14
  193.4 4.6 collective-permute-start.5
  198.3 26.5 %collective-permute-start.6 = (f32[2,2,2,256,128]{3,4,0,2,1:T(8,128)S(1)}, f32[2,2,2,256,128]{3,4,0,2,1:T(8,128)S(1)}, u32[]{:S(2)}, u32[]{:S(2)}) collective-permute-start(f32[2,2,2,256,128]{3,4,0,2,1:T(8,128)S(1)} %pad_maximum_fusion.6), channel_id=1, source_target_pairs={{0,32},{16,48},{32,0},{48,16},{64,96},{80,112},{96,64},{112,80},{1... | collective-permute-start | bytes 3145736 | tf_op jit(solution)/shard_map/ppermute | solution.py:14
  225.2 50.1 %collective-permute-start.7 = (f32[2,2,2,256,128]{3,4,0,2,1:T(8,128)S(1)}, f32[2,2,2,256,128]{3,4,0,2,1:T(8,128)S(1)}, u32[]{:S(2)}, u32[]{:S(2)}) collective-permute-start(f32[2,2,2,256,128]{3,4,0,2,1:T(8,128)S(1)} %pad_maximum_fusion.7), channel_id=1, source_target_pairs={{0,64},{16,80},{32,96},{48,112},{64,0},{80,16},{96,32},{112,48},{1... | collective-permute-start | bytes 3145736 | tf_op jit(solution)/shard_map/ppermute | solution.py:14
  275.7 52.7 %collective-permute-start.8 = (f32[2,2,2,256,128]{3,4,0,2,1:T(8,128)S(1)}, f32[2,2,2,256,128]{3,4,0,2,1:T(8,128)S(1)}, u32[]{:S(2)}, u32[]{:S(2)}) collective-permute-start(f32[2,2,2,256,128]{3,4,0,2,1:T(8,128)S(1)} %pad_maximum_fusion.8), channel_id=1, source_target_pairs={{0,128},{16,144},{32,160},{48,176},{64,192},{80,208},{96,224},{112... | collective-permute-start | bytes 3145736 | tf_op jit(solution)/shard_map/ppermute | solution.py:14
  328.7 29.5 %collective-permute-start.9 = (f32[2,2,2,256,128]{3,4,0,2,1:T(8,128)S(1)}, f32[2,2,2,256,128]{3,4,0,2,1:T(8,128)S(1)}, u32[]{:S(2)}, u32[]{:S(2)}) collective-permute-start(f32[2,2,2,256,128]{3,4,0,2,1:T(8,128)S(1)} %pad_maximum_fusion.9), channel_id=1, source_target_pairs={{0,256},{16,272},{32,288},{48,304},{64,320},{80,336},{96,352},{112... | collective-permute-start | bytes 3145736 | tf_op jit(solution)/shard_map/ppermute | solution.py:14
  358.5 35.4 %collective-permute-start.10 = (f32[2,1,2,256,128]{3,4,2,0,1:T(8,128)S(1)}, f32[2,1,2,256,128]{3,4,2,0,1:T(8,128)S(1)}, u32[]{:S(2)}, u32[]{:S(2)}) collective-permute-start(f32[2,1,2,256,128]{3,4,2,0,1:T(8,128)S(1)} %pad_bitcast_fusion), channel_id=1, source_target_pairs={{0,256},{16,272},{32,288},{48,304},{64,320},{80,336},{96,352},{112... | collective-permute-start | bytes 1572872 | tf_op jit(solution)/shard_map/ppermute | solution.py:14
  394.0 21.2 %collective-permute-start.11 = (f32[2,1,2,256,128]{3,4,2,1,0:T(8,128)S(1)}, f32[2,1,2,256,128]{3,4,2,1,0:T(8,128)S(1)}, u32[]{:S(2)}, u32[]{:S(2)}) collective-permute-start(f32[2,1,2,256,128]{3,4,2,1,0:T(8,128)S(1)} %pad_maximum_fusion.11), channel_id=1, source_target_pairs={{0,128},{16,144},{32,160},{48,176},{64,192},{80,208},{96,224},{112... | collective-permute-start | bytes 1572872 | tf_op jit(solution)/shard_map/ppermute | solution.py:14
  415.4 22.5 %collective-permute-start.12 = (f32[2,1,2,256,128]{3,4,2,1,0:T(8,128)S(1)}, f32[2,1,2,256,128]{3,4,2,1,0:T(8,128)S(1)}, u32[]{:S(2)}, u32[]{:S(2)}) collective-permute-start(f32[2,1,2,256,128]{3,4,2,1,0:T(8,128)S(1)} %pad_maximum_fusion.12), channel_id=1, source_target_pairs={{0,64},{16,80},{32,96},{48,112},{64,0},{80,16},{96,32},{112,48},{1... | collective-permute-start | bytes 1572872 | tf_op jit(solution)/shard_map/ppermute | solution.py:14
  438.0 14.9 %collective-permute-start.13 = (f32[2,1,2,256,128]{3,4,2,1,0:T(8,128)S(1)}, f32[2,1,2,256,128]{3,4,2,1,0:T(8,128)S(1)}, u32[]{:S(2)}, u32[]{:S(2)}) collective-permute-start(f32[2,1,2,256,128]{3,4,2,1,0:T(8,128)S(1)} %pad_maximum_fusion.13), channel_id=1, source_target_pairs={{0,32},{16,48},{32,0},{48,16},{64,96},{80,112},{96,64},{112,80},{1... | collective-permute-start | bytes 1572872 | tf_op jit(solution)/shard_map/ppermute | solution.py:14
  453.1 4.8 collective-permute-start.14
  460.3 3.8 collective-permute-start.15
  464.3 15.0 %collective-permute-start.16 = (f32[2,1,2,256,128]{3,4,2,1,0:T(8,128)S(1)}, f32[2,1,2,256,128]{3,4,2,1,0:T(8,128)S(1)}, u32[]{:S(2)}, u32[]{:S(2)}) collective-permute-start(f32[2,1,2,256,128]{3,4,2,1,0:T(8,128)S(1)} %pad_maximum_fusion.17), channel_id=1, source_target_pairs={{0,32},{16,48},{32,0},{48,16},{64,96},{80,112},{96,64},{112,80},{1... | collective-permute-start | bytes 1572872 | tf_op jit(solution)/shard_map/ppermute | solution.py:14
  479.5 27.6 %collective-permute-start.17 = (f32[2,1,2,256,128]{3,4,2,1,0:T(8,128)S(1)}, f32[2,1,2,256,128]{3,4,2,1,0:T(8,128)S(1)}, u32[]{:S(2)}, u32[]{:S(2)}) collective-permute-start(f32[2,1,2,256,128]{3,4,2,1,0:T(8,128)S(1)} %pad_maximum_fusion.18), channel_id=1, source_target_pairs={{0,64},{16,80},{32,96},{48,112},{64,0},{80,16},{96,32},{112,48},{1... | collective-permute-start | bytes 1572872 | tf_op jit(solution)/shard_map/ppermute | solution.py:14
  507.3 28.1 %collective-permute-start.18 = (f32[2,1,2,256,128]{3,4,2,1,0:T(8,128)S(1)}, f32[2,1,2,256,128]{3,4,2,1,0:T(8,128)S(1)}, u32[]{:S(2)}, u32[]{:S(2)}) collective-permute-start(f32[2,1,2,256,128]{3,4,2,1,0:T(8,128)S(1)} %pad_maximum_fusion.19), channel_id=1, source_target_pairs={{0,128},{16,144},{32,160},{48,176},{64,192},{80,208},{96,224},{112... | collective-permute-start | bytes 1572872 | tf_op jit(solution)/shard_map/ppermute | solution.py:14
  535.6 48.3 %collective-permute-start.19 = (f32[2,1,2,256,128]{3,4,2,1,0:T(8,128)S(1)}, f32[2,1,2,256,128]{3,4,2,1,0:T(8,128)S(1)}, u32[]{:S(2)}, u32[]{:S(2)}) collective-permute-start(f32[2,1,2,256,128]{3,4,2,1,0:T(8,128)S(1)} %pad_maximum_fusion.10), channel_id=1, source_target_pairs={{0,256},{16,272},{32,288},{48,304},{64,320},{80,336},{96,352},{112... | collective-permute-start | bytes 1572872 | tf_op jit(solution)/shard_map/ppermute | solution.py:14
  538.3 45.6 %collective-permute-start.20 = (f32[2,2,256,1]{2,3,1,0:T(1,128)S(1)}, f32[2,2,256,1]{2,3,1,0:T(1,128)S(1)}, u32[]{:S(2)}, u32[]{:S(2)}) collective-permute-start(f32[2,2,256,1]{2,3,1,0:T(1,128)S(1)} %get-tuple-element.49), channel_id=1, source_target_pairs={{1,0},{2,1},{3,2},{4,3},{5,4},{6,5},{7,6},{8,7},{9,8},{10,9},{11,1... | collective-permute-start | bytes 12296 | tf_op jit(solution)/shard_map/ppermute | solution.py:25
  539.6 44.3 %collective-permute-start.21 = (f32[2,2,256,1]{2,3,1,0:T(1,128)S(1)}, f32[2,2,256,1]{2,3,1,0:T(1,128)S(1)}, u32[]{:S(2)}, u32[]{:S(2)}) collective-permute-start(f32[2,2,256,1]{2,3,1,0:T(1,128)S(1)} %get-tuple-element.50), channel_id=1, source_target_pairs={{0,1},{1,2},{2,3},{3,4},{4,5},{5,6},{6,7},{7,8},{8,9},{9,10},{10,1... | collective-permute-start | bytes 12296 | tf_op jit(solution)/shard_map/ppermute | solution.py:24
where the time goes:
time: 587 us; the launch traced here: 585 us
  waiting for transfers between devices  408 us (70%)
  starting transfers between devices  152 us (26%)
  other arithmetic  13.4 us (2%)
    ppermute x20, waiting for transfers between devices, partner_2(): lax.ppermute(value, axis, [(i, i ^ 1 << bit) for i in range(lax.axis_size...  401 us
    ppermute x20, starting transfers between devices, partner_2(): lax.ppermute(value, axis, [(i, i ^ 1 << bit) for i in range(lax.axis_size...  112 us
    ppermute x1, starting transfers between devices, extended(): before = lax.ppermute(last, axis, up)  37.9 us
  transfers between devices with their start and end apart: 22, of which 19 were waited for; matrix products, arithmetic and copies ran while one was open for 1% of the time, Pallas kernels for 0%

commit v1 on v0

v1 whole, which is shorter than its diff:
```python
import functools
import math

import jax
import jax.numpy as jnp
import ml_dtypes
import numpy as np
from jax import lax
from jax.experimental import pallas as pl
from jax.experimental.pallas import tpu as pltpu
from jax.sharding import PartitionSpec as P

MESH = pl.DeviceIdType.MESH
conduction = 0.3
HALF = 128


def split_np(a):
    a32 = a.astype(np.float32)
    hi = a32.astype(ml_dtypes.bfloat16)
    lo = (a - hi.astype(np.float64)).astype(np.float32).astype(ml_dtypes.bfloat16)
    return hi, lo


@functools.lru_cache(maxsize=None)
def tables(n_dev, n_loc):
    total = n_dev * n_loc
    d = np.arange(n_dev)
    turn = -2.0 * np.pi * (np.outer(d, d) % n_dev) / n_dev
    c, s = np.cos(turn), np.sin(turn)
    outer = np.zeros((2, n_dev, 4, n_dev, 2, 4))
    for q in range(4):
        outer[0, :, q, :, 0, q] = c
        outer[0, :, q, :, 1, q] = -s
        outer[1, :, q, :, 0, q] = s
        outer[1, :, q, :, 1, q] = c
    outer = outer.reshape(8 * n_dev, 8 * n_dev)
    outer_inv = outer.T / n_dev
    j = np.arange(n_loc)
    turn = -2.0 * np.pi * (np.outer(j, j) % n_loc) / n_loc
    c, s = np.cos(turn), np.sin(turn)
    inner = np.block([[c, s], [-s, c]])
    inner_inv = inner.T / n_loc
    ka = np.repeat(d, 4)
    turn = -2.0 * np.pi * np.outer(ka, j) / total
    k = ka[:, None] + n_dev * j[None, :]
    signed = np.where(k < total // 2, k, k - total)
    kept = 3 * np.abs(signed) <= total
    wave = 2.0 * np.pi * signed / total
    first = np.where(2 * k == total, 0.0, wave)
    second = conduction * wave * wave * kept
    f32 = np.stack([np.cos(turn), np.sin(turn), kept, first, second]).astype(np.float32)
    mats = []
    for m in (outer, outer_inv):
        mats += split_np(m)
    big = []
    for m in (inner, inner_inv):
        big += split_np(m)
    return f32, np.stack(mats), np.stack(big)


def split(a):
    hi = a.astype(jnp.bfloat16)
    lo = (a - hi.astype(jnp.float32)).astype(jnp.bfloat16)
    return hi, lo


def dot(a, b):
    return jnp.dot(a, b, preferred_element_type=jnp.float32)


def kernel(
    n, layers,
    u_ref, w_ref, t_ref, f32_hbm, mats_hbm, big_hbm,
    out_ref,
    tab, mats, big, sbuf, rbuf, obuf, sspec, uphys, tphys, edge_s, edge_r,
    const_sem, send_sem, recv_sem, osend_sem, orecv_sem, esend_sem, erecv_sem,
):
    me = lax.axis_index("gx")
    lay = lax.axis_index("gz")
    blocks = n // 2
    b = lax.rem(me, blocks)
    base = me - b
    consts = [
        pltpu.make_async_copy(src, dst, const_sem.at[i])
        for i, (src, dst) in enumerate(((f32_hbm, tab), (mats_hbm, mats), (big_hbm, big)))
    ]
    for c in consts:
        c.start()
    nxt_gx = base + lax.rem(b + 1, blocks)
    nxt_gz = lax.rem(lay + jnp.where(b == blocks - 1, 1, 0), layers)
    prv_gx = base + lax.rem(b + blocks - 1, blocks)
    prv_gz = lax.rem(lay + jnp.where(b == 0, layers - 1, 0), layers)

    barrier = pltpu.get_barrier_semaphore()

    def greet(i, carry):
        pl.semaphore_signal(barrier, inc=1, device_id=(lax.rem(me + i, n), lay), device_id_type=MESH)
        return carry

    lax.fori_loop(1, n, greet, 0)
    pl.semaphore_signal(barrier, inc=1, device_id=(nxt_gx, nxt_gz), device_id_type=MESH)
    pl.semaphore_signal(barrier, inc=1, device_id=(prv_gx, prv_gz), device_id_type=MESH)

    def turned(src, f):
        for y in range(2):
            sbuf[f, pl.ds(y * blocks, blocks)] = src[y].T.reshape(blocks, 8, src.shape[1])

    def scatter(f):
        def send(i, carry):
            p = lax.rem(me + i, n)
            pltpu.make_async_remote_copy(
                src_ref=sbuf.at[f, p], dst_ref=rbuf.at[f, me],
                send_sem=send_sem.at[f], recv_sem=recv_sem.at[f],
                device_id=(p, lay), device_id_type=MESH,
            ).start()
            return carry

        lax.fori_loop(1, n, send, 0)
        pltpu.make_async_copy(sbuf.at[f, me], rbuf.at[f, me], recv_sem.at[f]).start()

    def gathered(f):
        pltpu.make_async_copy(sbuf.at[f], rbuf.at[f], recv_sem.at[f]).wait()

    turned(t_ref, 0)
    pl.semaphore_wait(barrier, n + 1)
    scatter(0)
    turned(u_ref, 1)
    scatter(1)
    turned(w_ref, 2)
    scatter(2)
    for c in consts:
        c.wait()

    def left(i, x):
        hi, lo = split(x)
        return dot(mats[i], hi) + dot(mats[i + 1], hi) + dot(mats[i], lo)

    def right(i, x):
        hi, lo = split(x)
        return dot(hi, big[i]) + dot(lo, big[i]) + dot(hi, big[i + 1])

    def forward(x):
        a = left(0, x)
        re, im = a[:HALF], a[HALF:]
        c, s = tab[0], tab[1]
        a = jnp.concatenate([re * c - im * s, re * s + im * c], axis=1)
        a = right(0, a)
        w = a.shape[1] // 2
        return a[:, :w], a[:, w:]

    def backward(re, im):
        a = right(2, jnp.concatenate([re, im], axis=1))
        w = a.shape[1] // 2
        re, im = a[:, :w], a[:, w:]
        c, s = tab[0], tab[1]
        a = jnp.concatenate([re * c + im * s, im * c - re * s], axis=0)
        return left(2, a)

    def lines(f):
        return rbuf[f].reshape(8 * n, rbuf.shape[3])

    def edges(i, value):
        v = value.reshape(n, 8, value.shape[1])
        edge_s[i, 0] = v[:, 0]
        edge_s[i, 1] = v[:, 7]

    def edge_copies(i):
        out = []
        for side, (gx, gz) in ((0, (prv_gx, prv_gz)), (1, (nxt_gx, nxt_gz))):
            out.append(pltpu.make_async_remote_copy(
                src_ref=edge_s.at[i, side], dst_ref=edge_r.at[i, side],
                send_sem=esend_sem.at[i, side], recv_sem=erecv_sem.at[i, side],
                device_id=(gx, gz), device_id_type=MESH,
            ))
        return out

    gathered(0)
    re, im = forward(lines(0))
    kept = tab[2]
    re, im = re * kept, im * kept
    sspec[0] = re
    sspec[1] = im
    tp = backward(re, im)
    tphys[...] = tp
    edges(0, tp)
    t_edges = edge_copies(0)
    for c in t_edges:
        c.start()
    gathered(1)
    re, im = forward(lines(1))
    kept = tab[2]
    up = backward(re * kept, im * kept)
    re, im = forward(up * tphys[...])
    first, second = tab[3], tab[4]
    uphys[...] = backward(first * im - second * sspec[0], -first * re - second * sspec[1])
    gathered(2)
    re, im = forward(lines(2))
    kept = tab[2]
    q = backward(re * kept, im * kept) * tphys[...]
    edges(1, q)
    q_edges = edge_copies(1)
    for c in q_edges:
        c.start()
    for c in t_edges + q_edges:
        c.wait()
    has_prev = jnp.where((b == 0) & (lay == 0), 0.0, 1.0).astype(jnp.float32)
    has_next = jnp.where((b == blocks - 1) & (lay == layers - 1), 0.0, 1.0).astype(jnp.float32)
    q3 = q.reshape(n, 8, q.shape[1])
    t3 = tphys[...].reshape(n, 8, q.shape[1])
    lower = jnp.concatenate([(0.5 * q3 + conduction * t3)[:, :7]], axis=1)
    upper = (conduction * t3 - 0.5 * q3)[:, 1:]
    low_edge = has_prev * (0.5 * edge_r[1, 1] + conduction * edge_r[0, 1])
    high_edge = has_next * (conduction * edge_r[0, 0] - 0.5 * edge_r[1, 0])
    h3 = uphys[...].reshape(n, 8, q.shape[1])
    total = h3 - 2.0 * conduction * t3
    total = total + jnp.concatenate([low_edge[:, None], lower], axis=1)
    total = total + jnp.concatenate([upper, high_edge[:, None]], axis=1)
    obuf[...] = total

    def send_back(i, carry):
        p = lax.rem(me + i, n)
        pltpu.make_async_remote_copy(
            src_ref=obuf.at[p], dst_ref=out_ref.at[me],
            send_sem=osend_sem.at[0], recv_sem=orecv_sem.at[0],
            device_id=(p, lay), device_id_type=MESH,
        ).start()
        return carry

    lax.fori_loop(1, n, send_back, 0)
    pltpu.make_async_copy(obuf.at[me], out_ref.at[me], orecv_sem.at[0]).start()
    pltpu.make_async_copy(obuf, out_ref, orecv_sem.at[0]).wait()

    some = pl.ds(0, n - 1)
    for f in range(3):
        pltpu.make_async_copy(sbuf.at[f, some], rbuf.at[f, some], send_sem.at[f]).wait()
    pltpu.make_async_copy(obuf.at[some], out_ref.at[some], osend_sem.at[0]).wait()


def solution(mesh):
    n = mesh.shape["gx"]
    layers = mesh.shape["gz"]

    def shards(u_field, w_field, temp_field):
        ys, nx, nz = u_field.shape
        f32, mats, big = (jnp.asarray(t) for t in tables(n, nx))
        vmem = pl.BlockSpec(memory_space=pltpu.VMEM)
        hbm = pl.BlockSpec(memory_space=pltpu.HBM)
        dma = pltpu.SemaphoreType.DMA
        back = pl.pallas_call(
            functools.partial(kernel, n, layers),
            out_shape=jax.ShapeDtypeStruct((n, 8, nx), jnp.float32),
            in_specs=[vmem] * 3 + [hbm] * 3,
            out_specs=vmem,
            scratch_shapes=[
                pltpu.VMEM(f32.shape, jnp.float32),
                pltpu.VMEM(mats.shape, jnp.bfloat16),
                pltpu.VMEM(big.shape, jnp.bfloat16),
                pltpu.VMEM((3, n, 8, nx), jnp.float32),
                pltpu.VMEM((3, n, 8, nx), jnp.float32),
                pltpu.VMEM((n, 8, nx), jnp.float32),
                pltpu.VMEM((2, HALF, nx), jnp.float32),
                pltpu.VMEM((8 * n, nx), jnp.float32),
                pltpu.VMEM((8 * n, nx), jnp.float32),
                pltpu.VMEM((2, 2, n, nx), jnp.float32),
                pltpu.VMEM((2, 2, n, nx), jnp.float32),
                dma((3,)), dma((3,)), dma((3,)), dma((1,)), dma((1,)), dma((2, 2)), dma((2, 2)),
            ],
            compiler_params=pltpu.CompilerParams(
                collective_id=0, has_side_effects=True, vmem_limit_bytes=40 * 2**20
            ),
        )(u_field, w_field, temp_field, f32, mats, big)
        return jnp.swapaxes(back.reshape(ys, nz, nx), 1, 2)

    spec = P(None, "gx", "gz")
    return jax.shard_map(shards, mesh=mesh, in_specs=(spec, spec, spec), out_specs=spec, check_vma=False)
```

time: 587 us -> 61.4 us (0.10)
  waiting for transfers between devices: 408 us -> 0 us
  starting transfers between devices: 152 us -> 0 us
  Pallas kernels: 0 us -> 53.7 us
  other arithmetic: 13.4 us -> 0 us
    ppermute x22 -> x0, waiting for transfers between devices: 408 us -> none  [the longest x20 401 us: partner_2(): lax.ppermute(value, axis, [(i, i ^ 1 << bit) for i in range(lax.axis_size...]
    ppermute x22 -> x0, starting transfers between devices: 152 us -> none  [the longest x20 112 us: partner_2(): lax.ppermute(value, axis, [(i, i ^ 1 << bit) for i in range(lax.axis_size...]
    pallas_call x0 -> x1, Pallas kernels: none -> 53.7 us  [shards(): pl.pallas_call(functools.partial(kernel, n, layers), out_shape=jax.ShapeD...]
  transfers between devices with their start and end apart: 22 -> 0, of which waited for: 19 -> 0; matrix products, arithmetic and copies ran while one was open for 1% -> 0% of each run, Pallas kernels for 0% -> 0%
where the time goes in v1:
time: 61.4 us; the launch traced here: 61.1 us
  Pallas kernels  53.7 us (87%)
  local copies, waits for them, and re-layouts  7.4 us (12%)
    pallas_call x1, Pallas kernels, shards(): pl.pallas_call(functools.partial(kernel, n, layers), out_shape=jax.ShapeD...  53.7 us
    unnamed x12, local copies, waits for them, and re-layouts  6.57 us

profile of v1, /device:TPU:1, one launch (start us, length us, event | category | flops | bytes accessed | tf_op | source)
XLA Modules:
  0.0 61.1 jit_solution(16766111169214299645)
XLA Ops:
  0.0 0.0 copy-start
  0.0 1.6 %copy-done = bf16[4,512,512]{2,1,0:T(8,128)(2,1)S(1)} copy-done((bf16[4,512,512]{2,1,0:T(8,128)(2,1)S(1)}, bf16[4,512,512]{2,1,0:T(8,128)(2,1)}, u32[]{:S(2)}) %copy-start) | copy-done | bytes 2097176
  1.6 0.0 copy-start.1
  1.6 1.1 %copy-done.1 = f32[5,128,256]{2,1,0:T(8,128)S(1)} copy-done((f32[5,128,256]{2,1,0:T(8,128)S(1)}, f32[5,128,256]{2,1,0:T(8,128)}, u32[]{:S(2)}) %copy-start.1) | copy-done | bytes 655384
  2.7 0.0 copy-start.2
  2.7 1.0 %copy-done.2 = bf16[4,256,256]{2,1,0:T(8,128)(2,1)S(1)} copy-done((bf16[4,256,256]{2,1,0:T(8,128)(2,1)S(1)}, bf16[4,256,256]{2,1,0:T(8,128)(2,1)}, u32[]{:S(2)}) %copy-start.2) | copy-done | bytes 524312
  3.7 0.0 copy-start.3
  3.7 0.9 %copy-done.3 = f32[2,256,128]{2,1,0:T(8,128)S(1)} copy-done((f32[2,256,128]{2,1,0:T(8,128)S(1)}, f32[2,256,128]{2,1,0:T(8,128)}, u32[]{:S(2)}) %copy-start.3) | copy-done | bytes 262168
  4.7 0.0 copy-start.4
  4.7 0.9 %copy-done.4 = f32[2,256,128]{2,1,0:T(8,128)S(1)} copy-done((f32[2,256,128]{2,1,0:T(8,128)S(1)}, f32[2,256,128]{2,1,0:T(8,128)}, u32[]{:S(2)}) %copy-start.4) | copy-done | bytes 262168
  5.6 0.0 copy-start.5
  5.6 0.9 %copy-done.5 = f32[2,256,128]{2,1,0:T(8,128)S(1)} copy-done((f32[2,256,128]{2,1,0:T(8,128)S(1)}, f32[2,256,128]{2,1,0:T(8,128)}, u32[]{:S(2)}) %copy-start.5) | copy-done | bytes 262168
  6.6 53.7 %shard_map.64 = f32[32,8,256]{2,1,0:T(8,128)S(1)} custom-call(f32[2,256,128]{2,1,0:T(8,128)S(1)} %copy-done.3, f32[2,256,128]{2,1,0:T(8,128)S(1)} %copy-done.4, f32[2,256,128]{2,1,0:T(8,128)S(1)} %copy-done.5, f32[5,128,256]{2,1,0:T(8,128)S(1)} %copy-done.1, bf16[4,256,256]{2,1,0:T(8,128)(2,1)S(1)} %copy-done.2, bf16[4,512,512]{2,1,0:T(8,128)(2,1)S(1)} %copy-done), custom_call_target="tpu_custom_call" | custom-call | tf_op jit(solution)/shard_map/pallas_call | solution.py:250
  60.3 0.8 %copy.7 = f32[2,128,256]{1,2,0:T(8,128)} copy(f32[2,128,256]{2,1,0:T(8,128)S(1)} %bitcast.2) | data formatting | bytes 524288 | tf_op jit(solution)/shard_map/reshape | solution.py:273
Async XLA Ops:
  0.0 1.6 %copy-start = (bf16[4,512,512]{2,1,0:T(8,128)(2,1)S(1)}, bf16[4,512,512]{2,1,0:T(8,128)(2,1)}, u32[]{:S(2)}) copy-start(bf16[4,512,512]{2,1,0:T(8,128)(2,1)} %constant.8.clone.big_hbm) | copy-start | bytes 6291460
  1.6 1.1 %copy-start.1 = (f32[5,128,256]{2,1,0:T(8,128)S(1)}, f32[5,128,256]{2,1,0:T(8,128)}, u32[]{:S(2)}) copy-start(f32[5,128,256]{2,1,0:T(8,128)} %constant.6.clone.f32_hbm) | copy-start | bytes 1966084
  2.7 1.0 %copy-start.2 = (bf16[4,256,256]{2,1,0:T(8,128)(2,1)S(1)}, bf16[4,256,256]{2,1,0:T(8,128)(2,1)}, u32[]{:S(2)}) copy-start(bf16[4,256,256]{2,1,0:T(8,128)(2,1)} %constant.7.clone.mats_hbm) | copy-start | bytes 1572868
  3.7 0.9 %copy-start.3 = (f32[2,256,128]{2,1,0:T(8,128)S(1)}, f32[2,256,128]{2,1,0:T(8,128)}, u32[]{:S(2)}) copy-start(f32[2,256,128]{2,1,0:T(8,128)} %u_ref.1) | copy-start | bytes 786436
  4.7 0.9 %copy-start.4 = (f32[2,256,128]{2,1,0:T(8,128)S(1)}, f32[2,256,128]{2,1,0:T(8,128)}, u32[]{:S(2)}) copy-start(f32[2,256,128]{2,1,0:T(8,128)} %w_ref.1) | copy-start | bytes 786436
  5.6 0.9 %copy-start.5 = (f32[2,256,128]{2,1,0:T(8,128)S(1)}, f32[2,256,128]{2,1,0:T(8,128)}, u32[]{:S(2)}) copy-start(f32[2,256,128]{2,1,0:T(8,128)} %t_ref.1) | copy-start | bytes 786436

commit v2 on v1

--- a/solution.py
+++ b/solution.py
@@ -71,10 +71,10 @@
 
 def kernel(
     n, layers,
-    u_ref, w_ref, t_ref, f32_hbm, mats_hbm, big_hbm,
+    u_hbm, w_hbm, t_hbm, f32_hbm, mats_hbm, big_hbm,
     out_ref,
-    tab, mats, big, sbuf, rbuf, obuf, sspec, uphys, tphys, edge_s, edge_r,
-    const_sem, send_sem, recv_sem, osend_sem, orecv_sem, esend_sem, erecv_sem,
+    fields, tab, mats, big, sbuf, rbuf, obuf, sspec, uphys, tphys, edge_s, edge_r,
+    load_sem, const_sem, send_sem, recv_sem, osend_sem, orecv_sem, esend_sem, erecv_sem,
 ):
     me = lax.axis_index("gx")
     lay = lax.axis_index("gz")
@@ -85,7 +85,11 @@
         pltpu.make_async_copy(src, dst, const_sem.at[i])
         for i, (src, dst) in enumerate(((f32_hbm, tab), (mats_hbm, mats), (big_hbm, big)))
     ]
-    for c in consts:
+    loads = [
+        pltpu.make_async_copy(src, fields.at[f], load_sem.at[f])
+        for f, src in enumerate((t_hbm, u_hbm, w_hbm))
+    ]
+    for c in loads + consts:
         c.start()
     nxt_gx = base + lax.rem(b + 1, blocks)
     nxt_gz = lax.rem(lay + jnp.where(b == blocks - 1, 1, 0), layers)
@@ -102,9 +106,10 @@
     pl.semaphore_signal(barrier, inc=1, device_id=(nxt_gx, nxt_gz), device_id_type=MESH)
     pl.semaphore_signal(barrier, inc=1, device_id=(prv_gx, prv_gz), device_id_type=MESH)
 
-    def turned(src, f):
+    def turned(f):
+        loads[f].wait()
         for y in range(2):
-            sbuf[f, pl.ds(y * blocks, blocks)] = src[y].T.reshape(blocks, 8, src.shape[1])
+            sbuf[f, pl.ds(y * blocks, blocks)] = fields[f, y].T.reshape(blocks, 8, fields.shape[2])
 
     def scatter(f):
         def send(i, carry):
@@ -122,12 +127,12 @@
     def gathered(f):
         pltpu.make_async_copy(sbuf.at[f], rbuf.at[f], recv_sem.at[f]).wait()
 
-    turned(t_ref, 0)
+    turned(0)
     pl.semaphore_wait(barrier, n + 1)
     scatter(0)
-    turned(u_ref, 1)
+    turned(1)
     scatter(1)
-    turned(w_ref, 2)
+    turned(2)
     scatter(2)
     for c in consts:
         c.wait()
@@ -250,9 +255,10 @@
         back = pl.pallas_call(
             functools.partial(kernel, n, layers),
             out_shape=jax.ShapeDtypeStruct((n, 8, nx), jnp.float32),
-            in_specs=[vmem] * 3 + [hbm] * 3,
+            in_specs=[hbm] * 6,
             out_specs=vmem,
             scratch_shapes=[
+                pltpu.VMEM((3, ys, nx, nz), jnp.float32),
                 pltpu.VMEM(f32.shape, jnp.float32),
                 pltpu.VMEM(mats.shape, jnp.bfloat16),
                 pltpu.VMEM(big.shape, jnp.bfloat16),
@@ -264,10 +270,10 @@
                 pltpu.VMEM((8 * n, nx), jnp.float32),
                 pltpu.VMEM((2, 2, n, nx), jnp.float32),
                 pltpu.VMEM((2, 2, n, nx), jnp.float32),
-                dma((3,)), dma((3,)), dma((3,)), dma((1,)), dma((1,)), dma((2, 2)), dma((2, 2)),
+                dma((3,)), dma((3,)), dma((3,)), dma((3,)), dma((1,)), dma((1,)), dma((2, 2)), dma((2, 2)),
             ],
             compiler_params=pltpu.CompilerParams(
-                collective_id=0, has_side_effects=True, vmem_limit_bytes=40 * 2**20
+                collective_id=0, has_side_effects=True, vmem_limit_bytes=60 * 2**20
             ),
         )(u_field, w_field, temp_field, f32, mats, big)
         return jnp.swapaxes(back.reshape(ys, nz, nx), 1, 2)

time: 61.4 us -> 56 us (0.912)
  local copies, waits for them, and re-layouts: 7.4 us -> 1.79 us
    unnamed x12 -> x0, local copies, waits for them, and re-layouts: 6.57 us -> none
    reshape x1, local copies, waits for them, and re-layouts: 0.84 us -> 1.79 us  [shards(): return jnp.swapaxes(back.reshape(ys, nz, nx), 1, 2)]
where the time goes in v2:
time: 56 us; the launch traced here: 55.8 us
  Pallas kernels  54 us (96%)
  local copies, waits for them, and re-layouts  1.79 us (3%)
    pallas_call x1, Pallas kernels, shards(): pl.pallas_call(functools.partial(kernel, n, layers), out_shape=jax.ShapeD...  54 us
    reshape x1, local copies, waits for them, and re-layouts, shards(): return jnp.swapaxes(back.reshape(ys, nz, nx), 1, 2)  1.79 us

profile of v2, /device:TPU:1, one launch (start us, length us, event | category | flops | bytes accessed | tf_op | source)
XLA Modules:
  0.0 55.8 jit_solution(9270138255779104197)
XLA Ops:
  0.0 54.0 %shard_map.64 = f32[32,8,256]{2,1,0:T(8,128)} custom-call(f32[2,256,128]{2,1,0:T(8,128)} %u_hbm.1, f32[2,256,128]{2,1,0:T(8,128)} %w_hbm.1, f32[2,256,128]{2,1,0:T(8,128)} %t_hbm.1, f32[5,128,256]{2,1,0:T(8,128)} %constant.6.clone.f32_hbm, bf16[4,256,256]{2,1,0:T(8,128)(2,1)} %constant.7.clone.mats_hbm, bf16[4,512,512]{2,1,0:T(8,128)(2,1)} %constant.8.clone.big_hbm), custom_call_target="tpu_custom_call" | custom-call | tf_op jit(solution)/shard_map/pallas_call | solution.py:255
  54.0 1.8 %copy.7 = f32[2,128,256]{1,2,0:T(8,128)} copy(f32[2,128,256]{2,1,0:T(8,128)} %bitcast.2) | data formatting | bytes 524288 | tf_op jit(solution)/shard_map/reshape | solution.py:279

commit v3 on v2

--- a/solution.py
+++ b/solution.py
@@ -12,7 +12,6 @@
 
 MESH = pl.DeviceIdType.MESH
 conduction = 0.3
-HALF = 128
 
 
 def split_np(a):
@@ -26,37 +25,59 @@
 def tables(n_dev, n_loc):
     total = n_dev * n_loc
     d = np.arange(n_dev)
-    turn = -2.0 * np.pi * (np.outer(d, d) % n_dev) / n_dev
+    k = d[:, None] + n_dev * np.arange(-n_loc // 2, n_loc // 2)[None, :]
+    kept = 3 * np.abs(k) <= total
+    count = kept.sum(1)
+    wide = count.max()
+    assert set(count) == {wide, wide - 1}
+    order = np.concatenate([d[count == wide], d[count < wide]])
+    n_wide = int((count == wide).sum())
+    low = np.argmax(kept, axis=1) - n_loc // 2
+    centre = low + (count - 1) / 2.0
+    turn = -2.0 * np.pi * (np.outer(order, d) % n_dev) / n_dev
     c, s = np.cos(turn), np.sin(turn)
-    outer = np.zeros((2, n_dev, 4, n_dev, 2, 4))
+    outer = np.zeros((n_dev, 2, 4, n_dev, 2, 4))
     for q in range(4):
-        outer[0, :, q, :, 0, q] = c
-        outer[0, :, q, :, 1, q] = -s
-        outer[1, :, q, :, 0, q] = s
-        outer[1, :, q, :, 1, q] = c
+        outer[:, 0, q, :, 0, q] = c
+        outer[:, 0, q, :, 1, q] = -s
+        outer[:, 1, q, :, 0, q] = s
+        outer[:, 1, q, :, 1, q] = c
     outer = outer.reshape(8 * n_dev, 8 * n_dev)
     outer_inv = outer.T / n_dev
     j = np.arange(n_loc)
-    turn = -2.0 * np.pi * (np.outer(j, j) % n_loc) / n_loc
-    c, s = np.cos(turn), np.sin(turn)
-    inner = np.block([[c, s], [-s, c]])
-    inner_inv = inner.T / n_loc
-    ka = np.repeat(d, 4)
-    turn = -2.0 * np.pi * np.outer(ka, j) / total
-    k = ka[:, None] + n_dev * j[None, :]
-    signed = np.where(k < total // 2, k, k - total)
-    kept = 3 * np.abs(signed) <= total
-    wave = 2.0 * np.pi * signed / total
-    first = np.where(2 * k == total, 0.0, wave)
-    second = conduction * wave * wave * kept
-    f32 = np.stack([np.cos(turn), np.sin(turn), kept, first, second]).astype(np.float32)
+    apart = 2.0 * np.pi * (j[None, :] - j[:, None]) / n_loc
+    step = 2.0 * np.pi / total
+
+    def real_kernels(modes):
+        kappa = np.arange(modes) - (modes - 1) / 2.0
+        angle = apart[..., None] * kappa
+        even = np.cos(angle).sum(-1) / n_loc
+        odd = -(kappa * np.sin(angle)).sum(-1) / n_loc
+        return even, odd * n_dev * step
+
+    def frame(offset):
+        turn = step * np.outer(order + n_dev * offset, j)
+        return np.cos(turn), np.sin(turn), np.repeat((order + n_dev * offset)[:, None], n_loc, 1) * step
+
+    def rows(a, signed):
+        a = np.repeat(a[:, None, :], 8, axis=1)
+        if signed:
+            a[:, :4] *= -1.0
+        return a.reshape(8 * n_dev, n_loc)
+
+    fc, fs, fa = frame(centre[order])
+    dc, ds, da = frame(np.full(n_dev, -0.5))
+    f32 = np.stack([
+        rows(fc, False), rows(fs, True), conduction * rows(fa, True),
+        rows(dc, False), rows(ds, True), rows(da, True),
+    ]).astype(np.float32)
+    even_w, odd_w = real_kernels(wide)
+    even_n, odd_n = real_kernels(wide - 1)
+    _, full = real_kernels(n_loc)
     mats = []
-    for m in (outer, outer_inv):
+    for m in (outer, outer_inv, even_w, conduction * odd_w, even_n, conduction * odd_n, full):
         mats += split_np(m)
-    big = []
-    for m in (inner, inner_inv):
-        big += split_np(m)
-    return f32, np.stack(mats), np.stack(big)
+    return f32, np.stack(mats), 8 * n_wide
 
 
 def split(a):
@@ -70,10 +91,10 @@
 
 
 def kernel(
-    n, layers,
-    u_hbm, w_hbm, t_hbm, f32_hbm, mats_hbm, big_hbm,
+    n, layers, cut,
+    u_hbm, w_hbm, t_hbm, f32_hbm, mats_hbm,
     out_ref,
-    fields, tab, mats, big, sbuf, rbuf, obuf, sspec, uphys, tphys, edge_s, edge_r,
+    fields, tab, mats, sbuf, rbuf, obuf, grad, tphys, qphys, vert, edge_s, edge_r,
     load_sem, const_sem, send_sem, recv_sem, osend_sem, orecv_sem, esend_sem, erecv_sem,
 ):
     me = lax.axis_index("gx")
@@ -83,11 +104,11 @@
     base = me - b
     consts = [
         pltpu.make_async_copy(src, dst, const_sem.at[i])
-        for i, (src, dst) in enumerate(((f32_hbm, tab), (mats_hbm, mats), (big_hbm, big)))
+        for i, (src, dst) in enumerate(((f32_hbm, tab), (mats_hbm, mats)))
     ]
     loads = [
         pltpu.make_async_copy(src, fields.at[f], load_sem.at[f])
-        for f, src in enumerate((t_hbm, u_hbm, w_hbm))
+        for f, src in enumerate((t_hbm, w_hbm, u_hbm))
     ]
     for c in loads + consts:
         c.start()
@@ -141,26 +162,52 @@
         hi, lo = split(x)
         return dot(mats[i], hi) + dot(mats[i + 1], hi) + dot(mats[i], lo)
 
-    def right(i, x):
+    def right(i, hi, lo):
+        return dot(hi, mats[i]) + dot(lo, mats[i]) + dot(hi, mats[i + 1])
+
+    def swapped(x):
+        x3 = x.reshape(n, 8, x.shape[1])
+        return jnp.concatenate([x3[:, 4:], x3[:, :4]], axis=1).reshape(x.shape)
+
+    def modulated(x, i):
+        return x * tab[i] - swapped(x) * tab[i + 1]
+
+    def demodulated(x, i):
+        return x * tab[i] + swapped(x) * tab[i + 1]
+
+    low_cut, high_cut = cut // 16 * 16, -(-cut // 16) * 16
+
+    def by_class(x, i):
         hi, lo = split(x)
-        return dot(hi, big[i]) + dot(lo, big[i]) + dot(hi, big[i + 1])
-
-    def forward(x):
+        first = right(i, hi[:high_cut], lo[:high_cut])
+        second = right(i + 4, hi[low_cut:], lo[low_cut:])
+        return jnp.concatenate([first[:cut], second[cut - low_cut:]], axis=0)
+
+    def filtered(x):
+        a = modulated(left(0, x), 0)
+        return left(2, demodulated(by_class(a, 4), 0))
+
+    def filtered_and_gradient(x):
+        a = modulated(left(0, x), 0)
+        kept = demodulated(by_class(a, 4), 0)
+        slope = demodulated(by_class(a, 6), 0) + swapped(kept) * tab[2]
+        both = left(2, jnp.concatenate([kept, slope], axis=1))
+        w = both.shape[1] // 2
+        return both[:, :w], both[:, w:]
+
+    def gradient(x):
         a = left(0, x)
-        re, im = a[:HALF], a[HALF:]
-        c, s = tab[0], tab[1]
-        a = jnp.concatenate([re * c - im * s, re * s + im * c], axis=1)
-        a = right(0, a)
-        w = a.shape[1] // 2
-        return a[:, :w], a[:, w:]
-
-    def backward(re, im):
-        a = right(2, jnp.concatenate([re, im], axis=1))
-        w = a.shape[1] // 2
-        re, im = a[:, :w], a[:, w:]
-        c, s = tab[0], tab[1]
-        a = jnp.concatenate([re * c + im * s, im * c - re * s], axis=0)
-        return left(2, a)
+        hi, lo = split(modulated(a, 3))
+        b = demodulated(right(12, hi, lo), 3) + swapped(a) * tab[5]
+        lane = lax.broadcasted_iota(jnp.int32, (8, a.shape[1]), 1)
+        sign = jnp.where(lane % 2 == 0, 1.0, -1.0).astype(jnp.float32)
+        total = jnp.sum(a[:8] * sign, axis=1, keepdims=True) * (math.pi / a.shape[1])
+        part = lax.broadcasted_iota(jnp.int32, (8, a.shape[1]), 0)
+        total = jnp.broadcast_to(total, sign.shape)
+        turned_total = jnp.concatenate([total[4:], total[:4]], axis=0)
+        fix = jnp.where(part < 4, -turned_total, turned_total) * sign
+        b = jnp.concatenate([b[:8] + fix, b[8:]], axis=0)
+        return left(2, b)
 
     def lines(f):
         return rbuf[f].reshape(8 * n, rbuf.shape[3])
@@ -181,28 +228,16 @@
         return out
 
     gathered(0)
-    re, im = forward(lines(0))
-    kept = tab[2]
-    re, im = re * kept, im * kept
-    sspec[0] = re
-    sspec[1] = im
-    tp = backward(re, im)
+    tp, slope = filtered_and_gradient(lines(0))
     tphys[...] = tp
+    grad[...] = slope
     edges(0, tp)
     t_edges = edge_copies(0)
     for c in t_edges:
         c.start()
     gathered(1)
-    re, im = forward(lines(1))
-    kept = tab[2]
-    up = backward(re * kept, im * kept)
-    re, im = forward(up * tphys[...])
-    first, second = tab[3], tab[4]
-    uphys[...] = backward(first * im - second * sspec[0], -first * re - second * sspec[1])
-    gathered(2)
-    re, im = forward(lines(2))
-    kept = tab[2]
-    q = backward(re * kept, im * kept) * tphys[...]
+    q = filtered(lines(1)) * tphys[...]
+    qphys[...] = q
     edges(1, q)
     q_edges = edge_copies(1)
     for c in q_edges:
@@ -211,17 +246,18 @@
         c.wait()
     has_prev = jnp.where((b == 0) & (lay == 0), 0.0, 1.0).astype(jnp.float32)
     has_next = jnp.where((b == blocks - 1) & (lay == layers - 1), 0.0, 1.0).astype(jnp.float32)
-    q3 = q.reshape(n, 8, q.shape[1])
+    q3 = qphys[...].reshape(n, 8, q.shape[1])
     t3 = tphys[...].reshape(n, 8, q.shape[1])
-    lower = jnp.concatenate([(0.5 * q3 + conduction * t3)[:, :7]], axis=1)
+    lower = (0.5 * q3 + conduction * t3)[:, :7]
     upper = (conduction * t3 - 0.5 * q3)[:, 1:]
     low_edge = has_prev * (0.5 * edge_r[1, 1] + conduction * edge_r[0, 1])
     high_edge = has_next * (conduction * edge_r[0, 0] - 0.5 * edge_r[1, 0])
-    h3 = uphys[...].reshape(n, 8, q.shape[1])
-    total = h3 - 2.0 * conduction * t3
-    total = total + jnp.concatenate([low_edge[:, None], lower], axis=1)
-    total = total + jnp.concatenate([upper, high_edge[:, None]], axis=1)
-    obuf[...] = total
+    total = jnp.concatenate([low_edge[:, None], lower], axis=1) - 2.0 * conduction * t3
+    vert[...] = total + jnp.concatenate([upper, high_edge[:, None]], axis=1)
+    gathered(2)
+    flux = filtered(lines(2)) * tphys[...]
+    across = gradient(grad[...] - flux)
+    obuf[...] = across.reshape(obuf.shape) + vert[...]
 
     def send_back(i, carry):
         p = lax.rem(me + i, n)
@@ -248,34 +284,35 @@
 
     def shards(u_field, w_field, temp_field):
         ys, nx, nz = u_field.shape
-        f32, mats, big = (jnp.asarray(t) for t in tables(n, nx))
+        f32, mats, cut = tables(n, nx)
+        f32, mats = jnp.asarray(f32), jnp.asarray(mats)
         vmem = pl.BlockSpec(memory_space=pltpu.VMEM)
         hbm = pl.BlockSpec(memory_space=pltpu.HBM)
         dma = pltpu.SemaphoreType.DMA
         back = pl.pallas_call(
-            functools.partial(kernel, n, layers),
+            functools.partial(kernel, n, layers, cut),
             out_shape=jax.ShapeDtypeStruct((n, 8, nx), jnp.float32),
-            in_specs=[hbm] * 6,
+            in_specs=[hbm] * 5,
             out_specs=vmem,
             scratch_shapes=[
                 pltpu.VMEM((3, ys, nx, nz), jnp.float32),
                 pltpu.VMEM(f32.shape, jnp.float32),
                 pltpu.VMEM(mats.shape, jnp.bfloat16),
-                pltpu.VMEM(big.shape, jnp.bfloat16),
                 pltpu.VMEM((3, n, 8, nx), jnp.float32),
                 pltpu.VMEM((3, n, 8, nx), jnp.float32),
                 pltpu.VMEM((n, 8, nx), jnp.float32),
-                pltpu.VMEM((2, HALF, nx), jnp.float32),
                 pltpu.VMEM((8 * n, nx), jnp.float32),
                 pltpu.VMEM((8 * n, nx), jnp.float32),
+                pltpu.VMEM((8 * n, nx), jnp.float32),
+                pltpu.VMEM((n, 8, nx), jnp.float32),
                 pltpu.VMEM((2, 2, n, nx), jnp.float32),
                 pltpu.VMEM((2, 2, n, nx), jnp.float32),
-                dma((3,)), dma((3,)), dma((3,)), dma((3,)), dma((1,)), dma((1,)), dma((2, 2)), dma((2, 2)),
+                dma((3,)), dma((2,)), dma((3,)), dma((3,)), dma((1,)), dma((1,)), dma((2, 2)), dma((2, 2)),
             ],
             compiler_params=pltpu.CompilerParams(
                 collective_id=0, has_side_effects=True, vmem_limit_bytes=60 * 2**20
             ),
-        )(u_field, w_field, temp_field, f32, mats, big)
+        )(u_field, w_field, temp_field, f32, mats)
         return jnp.swapaxes(back.reshape(ys, nz, nx), 1, 2)
 
     spec = P(None, "gx", "gz")

time: 56 us -> 52.9 us (0.945)
  Pallas kernels: 54 us -> 51 us
    pallas_call x1, Pallas kernels: 54 us -> 51 us  [shards(): pl.pallas_call(functools.partial(kernel, n, layers, cut), out_shape=jax.S...]
where the time goes in v3:
time: 52.9 us; the launch traced here: 52.8 us
  Pallas kernels  51 us (96%)
  local copies, waits for them, and re-layouts  1.79 us (3%)
    pallas_call x1, Pallas kernels, shards(): pl.pallas_call(functools.partial(kernel, n, layers, cut), out_shape=jax.S...  51 us
    reshape x1, local copies, waits for them, and re-layouts, shards(): return jnp.swapaxes(back.reshape(ys, nz, nx), 1, 2)  1.79 us

profile of v3, /device:TPU:1, one launch (start us, length us, event | category | flops | bytes accessed | tf_op | source)
XLA Modules:
  0.0 52.8 jit_solution(5360389731530308679)
XLA Ops:
  0.0 51.0 %shard_map.55 = f32[32,8,256]{2,1,0:T(8,128)} custom-call(f32[2,256,128]{2,1,0:T(8,128)} %u_hbm.1, f32[2,256,128]{2,1,0:T(8,128)} %w_hbm.1, f32[2,256,128]{2,1,0:T(8,128)} %t_hbm.1, f32[6,256,256]{2,1,0:T(8,128)} %constant.4.clone.f32_hbm, bf16[14,256,256]{2,1,0:T(8,128)(2,1)} %constant.5.clone.mats_hbm), custom_call_target="tpu_custom_call" | custom-call | tf_op jit(solution)/shard_map/pallas_call | solution.py:292
  51.0 1.8 %copy.6 = f32[2,128,256]{1,2,0:T(8,128)} copy(f32[2,128,256]{2,1,0:T(8,128)} %bitcast.2) | data formatting | bytes 524288 | tf_op jit(solution)/shard_map/reshape | solution.py:316

commit v4 on v3

--- a/solution.py
+++ b/solution.py
@@ -291,7 +291,7 @@
         dma = pltpu.SemaphoreType.DMA
         back = pl.pallas_call(
             functools.partial(kernel, n, layers, cut),
-            out_shape=jax.ShapeDtypeStruct((n, 8, nx), jnp.float32),
+            out_shape=pltpu.VMEM((n, 8, nx), jnp.float32),
             in_specs=[hbm] * 5,
             out_specs=vmem,
             scratch_shapes=[

time: 52.9 us -> 51.2 us (0.968)
  local copies, waits for them, and re-layouts: 1.79 us -> 0.84 us
  Pallas kernels: 51 us -> 50.3 us
    reshape x1, local copies, waits for them, and re-layouts: 1.79 us -> 0.84 us  [shards(): return jnp.swapaxes(back.reshape(ys, nz, nx), 1, 2)]
    pallas_call x1, Pallas kernels: 51 us -> 50.3 us  [shards(): pl.pallas_call(functools.partial(kernel, n, layers, cut), out_shape=pltpu...]
where the time goes in v4:
time: 51.2 us; the launch traced here: 51.1 us
  Pallas kernels  50.3 us (98%)
  local copies, waits for them, and re-layouts  0.84 us (2%)
    pallas_call x1, Pallas kernels, shards(): pl.pallas_call(functools.partial(kernel, n, layers, cut), out_shape=pltpu...  50.3 us

profile of v4, /device:TPU:1, one launch (start us, length us, event | category | flops | bytes accessed | tf_op | source)
XLA Modules:
  0.0 51.1 jit_solution(7679356274521322033)
XLA Ops:
  0.0 50.3 %shard_map.55 = f32[32,8,256]{2,1,0:T(8,128)S(1)} custom-call(f32[2,256,128]{2,1,0:T(8,128)} %u_hbm.1, f32[2,256,128]{2,1,0:T(8,128)} %w_hbm.1, f32[2,256,128]{2,1,0:T(8,128)} %t_hbm.1, f32[6,256,256]{2,1,0:T(8,128)} %constant.4.clone.f32_hbm, bf16[14,256,256]{2,1,0:T(8,128)(2,1)} %constant.5.clone.mats_hbm), custom_call_target="tpu_custom_call" | custom-call | tf_op jit(solution)/shard_map/pallas_call | solution.py:292
  50.3 0.8 %copy.6 = f32[2,128,256]{1,2,0:T(8,128)} copy(f32[2,128,256]{2,1,0:T(8,128)S(1)} %bitcast.2) | data formatting | bytes 524288 | tf_op jit(solution)/shard_map/reshape | solution.py:316

commit v5 on v4

--- a/solution.py
+++ b/solution.py
@@ -94,7 +94,7 @@
     n, layers, cut,
     u_hbm, w_hbm, t_hbm, f32_hbm, mats_hbm,
     out_ref,
-    fields, tab, mats, sbuf, rbuf, obuf, grad, tphys, qphys, vert, edge_s, edge_r,
+    fields, tab, mats, sbuf, rbuf, obuf, grad, tphys, vert, edge_s, edge_r,
     load_sem, const_sem, send_sem, recv_sem, osend_sem, orecv_sem, esend_sem, erecv_sem,
 ):
     me = lax.axis_index("gx")
@@ -134,7 +134,7 @@
 
     def scatter(f):
         def send(i, carry):
-            p = lax.rem(me + i, n)
+            p = lax.rem(me + n - i, n)
             pltpu.make_async_remote_copy(
                 src_ref=sbuf.at[f, p], dst_ref=rbuf.at[f, me],
                 send_sem=send_sem.at[f], recv_sem=recv_sem.at[f],
@@ -195,7 +195,7 @@
         w = both.shape[1] // 2
         return both[:, :w], both[:, w:]
 
-    def gradient(x):
+    def gradient_spectrum(x):
         a = left(0, x)
         hi, lo = split(modulated(a, 3))
         b = demodulated(right(12, hi, lo), 3) + swapped(a) * tab[5]
@@ -206,8 +206,7 @@
         total = jnp.broadcast_to(total, sign.shape)
         turned_total = jnp.concatenate([total[4:], total[:4]], axis=0)
         fix = jnp.where(part < 4, -turned_total, turned_total) * sign
-        b = jnp.concatenate([b[:8] + fix, b[8:]], axis=0)
-        return left(2, b)
+        return jnp.concatenate([b[:8] + fix, b[8:]], axis=0)
 
     def lines(f):
         return rbuf[f].reshape(8 * n, rbuf.shape[3])
@@ -237,26 +236,26 @@
         c.start()
     gathered(1)
     q = filtered(lines(1)) * tphys[...]
-    qphys[...] = q
     edges(1, q)
     q_edges = edge_copies(1)
     for c in q_edges:
         c.start()
+    q3 = q.reshape(n, 8, q.shape[1])
+    t3 = tphys[...].reshape(n, 8, q.shape[1])
+    none = jnp.zeros((n, 1, q.shape[1]), jnp.float32)
+    lower = jnp.concatenate([none, (0.5 * q3 + conduction * t3)[:, :7]], axis=1)
+    higher = jnp.concatenate([(conduction * t3 - 0.5 * q3)[:, 1:], none], axis=1)
+    vert[...] = lower - 2.0 * conduction * t3 + higher
+    gathered(2)
+    flux = filtered(lines(2)) * tphys[...]
+    spec_hi, spec_lo = split(gradient_spectrum(grad[...] - flux))
     for c in t_edges + q_edges:
         c.wait()
     has_prev = jnp.where((b == 0) & (lay == 0), 0.0, 1.0).astype(jnp.float32)
     has_next = jnp.where((b == blocks - 1) & (lay == layers - 1), 0.0, 1.0).astype(jnp.float32)
-    q3 = qphys[...].reshape(n, 8, q.shape[1])
-    t3 = tphys[...].reshape(n, 8, q.shape[1])
-    lower = (0.5 * q3 + conduction * t3)[:, :7]
-    upper = (conduction * t3 - 0.5 * q3)[:, 1:]
-    low_edge = has_prev * (0.5 * edge_r[1, 1] + conduction * edge_r[0, 1])
-    high_edge = has_next * (conduction * edge_r[0, 0] - 0.5 * edge_r[1, 0])
-    total = jnp.concatenate([low_edge[:, None], lower], axis=1) - 2.0 * conduction * t3
-    vert[...] = total + jnp.concatenate([upper, high_edge[:, None]], axis=1)
-    gathered(2)
-    flux = filtered(lines(2)) * tphys[...]
-    across = gradient(grad[...] - flux)
+    vert[:, 0] += has_prev * (0.5 * edge_r[1, 1] + conduction * edge_r[0, 1])
+    vert[:, 7] += has_next * (conduction * edge_r[0, 0] - 0.5 * edge_r[1, 0])
+    across = dot(mats[2], spec_hi) + dot(mats[3], spec_hi) + dot(mats[2], spec_lo)
     obuf[...] = across.reshape(obuf.shape) + vert[...]
 
     def send_back(i, carry):
@@ -303,7 +302,6 @@
                 pltpu.VMEM((n, 8, nx), jnp.float32),
                 pltpu.VMEM((8 * n, nx), jnp.float32),
                 pltpu.VMEM((8 * n, nx), jnp.float32),
-                pltpu.VMEM((8 * n, nx), jnp.float32),
                 pltpu.VMEM((n, 8, nx), jnp.float32),
                 pltpu.VMEM((2, 2, n, nx), jnp.float32),
                 pltpu.VMEM((2, 2, n, nx), jnp.float32),

time: 51.2 us -> 48.8 us (0.953)
  Pallas kernels: 50.3 us -> 47.9 us
    pallas_call x1, Pallas kernels: 50.3 us -> 47.9 us  [shards(): pl.pallas_call(functools.partial(kernel, n, layers, cut), out_shape=pltpu...]
where the time goes in v5:
time: 48.8 us; the launch traced here: 48.7 us
  Pallas kernels  47.9 us (98%)
  local copies, waits for them, and re-layouts  0.84 us (2%)
    pallas_call x1, Pallas kernels, shards(): pl.pallas_call(functools.partial(kernel, n, layers, cut), out_shape=pltpu...  47.9 us

profile of v5, /device:TPU:1, one launch (start us, length us, event | category | flops | bytes accessed | tf_op | source)
XLA Modules:
  0.0 48.7 jit_solution(14577711066217880925)
XLA Ops:
  0.0 47.9 %shard_map.55 = f32[32,8,256]{2,1,0:T(8,128)S(1)} custom-call(f32[2,256,128]{2,1,0:T(8,128)} %u_hbm.1, f32[2,256,128]{2,1,0:T(8,128)} %w_hbm.1, f32[2,256,128]{2,1,0:T(8,128)} %t_hbm.1, f32[6,256,256]{2,1,0:T(8,128)} %constant.4.clone.f32_hbm, bf16[14,256,256]{2,1,0:T(8,128)(2,1)} %constant.5.clone.mats_hbm), custom_call_target="tpu_custom_call" | custom-call | tf_op jit(solution)/shard_map/pallas_call | solution.py:291
  47.9 0.8 %copy.6 = f32[2,128,256]{1,2,0:T(8,128)} copy(f32[2,128,256]{2,1,0:T(8,128)S(1)} %bitcast.2) | data formatting | bytes 524288 | tf_op jit(solution)/shard_map/reshape | solution.py:314

commit v6 on v5

--- a/solution.py
+++ b/solution.py
@@ -94,7 +94,7 @@
     n, layers, cut,
     u_hbm, w_hbm, t_hbm, f32_hbm, mats_hbm,
     out_ref,
-    fields, tab, mats, sbuf, rbuf, obuf, grad, tphys, vert, edge_s, edge_r,
+    fields, tab, mats, sbuf, rbuf, obuf, back, grad, tphys, vert, edge_s, edge_r,
     load_sem, const_sem, send_sem, recv_sem, osend_sem, orecv_sem, esend_sem, erecv_sem,
 ):
     me = lax.axis_index("gx")
@@ -132,18 +132,30 @@
         for y in range(2):
             sbuf[f, pl.ds(y * blocks, blocks)] = fields[f, y].T.reshape(blocks, 8, fields.shape[2])
 
-    def scatter(f):
-        def send(i, carry):
-            p = lax.rem(me + n - i, n)
+    half = 4
+
+    def to_peers(src, dst, send_s, recv_s, sign):
+        def step(i, carry):
+            p = lax.rem(me + n + sign * i, n)
             pltpu.make_async_remote_copy(
-                src_ref=sbuf.at[f, p], dst_ref=rbuf.at[f, me],
-                send_sem=send_sem.at[f], recv_sem=recv_sem.at[f],
+                src_ref=src(p), dst_ref=dst(me), send_sem=send_s, recv_sem=recv_s,
                 device_id=(p, lay), device_id_type=MESH,
             ).start()
             return carry
 
-        lax.fori_loop(1, n, send, 0)
-        pltpu.make_async_copy(sbuf.at[f, me], rbuf.at[f, me], recv_sem.at[f]).start()
+        lax.fori_loop(1, n, step, 0)
+        pltpu.make_async_copy(src(me), dst(me), recv_s).start()
+
+    def scatter(f):
+        to_peers(lambda p: sbuf.at[f, p], lambda p: rbuf.at[f, p], send_sem.at[f], recv_sem.at[f], -1)
+
+    def scatter_half(f, c):
+        part = pl.ds(half * c, half)
+        to_peers(lambda p: sbuf.at[f, p, part], lambda p: rbuf.at[f, p, part], send_sem.at[f + c], recv_sem.at[f + c], -1)
+
+    def gathered_half(f, c):
+        part = pl.ds(half * c, half)
+        pltpu.make_async_copy(sbuf.at[f, :, part], rbuf.at[f, :, part], recv_sem.at[f + c]).wait()
 
     def gathered(f):
         pltpu.make_async_copy(sbuf.at[f], rbuf.at[f], recv_sem.at[f]).wait()
@@ -154,7 +166,8 @@
     turned(1)
     scatter(1)
     turned(2)
-    scatter(2)
+    scatter_half(2, 0)
+    scatter_half(2, 1)
     for c in consts:
         c.wait()
 
@@ -246,35 +259,51 @@
     lower = jnp.concatenate([none, (0.5 * q3 + conduction * t3)[:, :7]], axis=1)
     higher = jnp.concatenate([(conduction * t3 - 0.5 * q3)[:, 1:], none], axis=1)
     vert[...] = lower - 2.0 * conduction * t3 + higher
-    gathered(2)
-    flux = filtered(lines(2)) * tphys[...]
-    spec_hi, spec_lo = split(gradient_spectrum(grad[...] - flux))
-    for c in t_edges + q_edges:
-        c.wait()
-    has_prev = jnp.where((b == 0) & (lay == 0), 0.0, 1.0).astype(jnp.float32)
-    has_next = jnp.where((b == blocks - 1) & (lay == layers - 1), 0.0, 1.0).astype(jnp.float32)
-    vert[:, 0] += has_prev * (0.5 * edge_r[1, 1] + conduction * edge_r[0, 1])
-    vert[:, 7] += has_next * (conduction * edge_r[0, 0] - 0.5 * edge_r[1, 0])
-    across = dot(mats[2], spec_hi) + dot(mats[3], spec_hi) + dot(mats[2], spec_lo)
-    obuf[...] = across.reshape(obuf.shape) + vert[...]
-
-    def send_back(i, carry):
-        p = lax.rem(me + i, n)
-        pltpu.make_async_remote_copy(
-            src_ref=obuf.at[p], dst_ref=out_ref.at[me],
-            send_sem=osend_sem.at[0], recv_sem=orecv_sem.at[0],
-            device_id=(p, lay), device_id_type=MESH,
-        ).start()
-        return carry
-
-    lax.fori_loop(1, n, send_back, 0)
-    pltpu.make_async_copy(obuf.at[me], out_ref.at[me], orecv_sem.at[0]).start()
-    pltpu.make_async_copy(obuf, out_ref, orecv_sem.at[0]).wait()
+    def alone(x, c):
+        zero = jnp.zeros(x.shape, x.dtype)
+        parts = [x, zero] if c == 0 else [zero, x]
+        return jnp.concatenate(parts, axis=1).reshape(8 * n, x.shape[2])
+
+    def half_of(x, c):
+        return x.reshape(n, 8, x.shape[-1])[:, half * c: half * c + half]
+
+    for part in range(2):
+        rows = slice(half * part, half * part + half)
+        gathered_half(2, part)
+        flux = half_of(filtered(alone(rbuf[2, :, rows], part)), part) * half_of(tphys[...], part)
+        hi, lo = split(gradient_spectrum(alone(half_of(grad[...], part) - flux, part)))
+        across = dot(mats[2], hi) + dot(mats[3], hi) + dot(mats[2], lo)
+        if part == 0:
+            for c in t_edges + q_edges:
+                c.wait()
+            has_prev = jnp.where((b == 0) & (lay == 0), 0.0, 1.0).astype(jnp.float32)
+            has_next = jnp.where((b == blocks - 1) & (lay == layers - 1), 0.0, 1.0).astype(jnp.float32)
+            vert[:, 0] += has_prev * (0.5 * edge_r[1, 1] + conduction * edge_r[0, 1])
+            vert[:, 7] += has_next * (conduction * edge_r[0, 0] - 0.5 * edge_r[1, 0])
+
+        done = half_of(across, part) + vert[:, rows]
+        mid = done.shape[2] // 2
+        obuf[part] = jnp.concatenate([done[:, :, :mid], done[:, :, mid:]], axis=1)
+        to_peers(lambda p: obuf.at[part, p], lambda p: back.at[part, p], osend_sem.at[part], orecv_sem.at[0], 1)
+
+    pltpu.make_async_copy(obuf, back, orecv_sem.at[0]).wait()
+    for y in range(2):
+        peers = slice(y * blocks, (y + 1) * blocks)
+        cols = [
+            jnp.concatenate([back[c, peers, half * side: half * side + half] for c in range(2)], axis=1)
+            for side in range(2)
+        ]
+        lines_z = jnp.concatenate(cols, axis=2)
+        out_ref[y] = lines_z.reshape(8 * blocks, lines_z.shape[2]).T
 
     some = pl.ds(0, n - 1)
-    for f in range(3):
+    for f in range(2):
         pltpu.make_async_copy(sbuf.at[f, some], rbuf.at[f, some], send_sem.at[f]).wait()
-    pltpu.make_async_copy(obuf.at[some], out_ref.at[some], osend_sem.at[0]).wait()
+    for c in range(2):
+        span = pl.ds(half * c, half)
+        pltpu.make_async_copy(sbuf.at[2, some, span], rbuf.at[2, some, span], send_sem.at[2 + c]).wait()
+    for c in range(2):
+        pltpu.make_async_copy(obuf.at[c, some], back.at[c, some], osend_sem.at[c]).wait()
 
 
 def solution(mesh):
@@ -288,9 +317,9 @@
         vmem = pl.BlockSpec(memory_space=pltpu.VMEM)
         hbm = pl.BlockSpec(memory_space=pltpu.HBM)
         dma = pltpu.SemaphoreType.DMA
-        back = pl.pallas_call(
+        return pl.pallas_call(
             functools.partial(kernel, n, layers, cut),
-            out_shape=pltpu.VMEM((n, 8, nx), jnp.float32),
+            out_shape=pltpu.VMEM((ys, nx, nz), jnp.float32),
             in_specs=[hbm] * 5,
             out_specs=vmem,
             scratch_shapes=[
@@ -299,19 +328,19 @@
                 pltpu.VMEM(mats.shape, jnp.bfloat16),
                 pltpu.VMEM((3, n, 8, nx), jnp.float32),
                 pltpu.VMEM((3, n, 8, nx), jnp.float32),
-                pltpu.VMEM((n, 8, nx), jnp.float32),
+                pltpu.VMEM((2, n, 8, nx // 2), jnp.float32),
+                pltpu.VMEM((2, n, 8, nx // 2), jnp.float32),
                 pltpu.VMEM((8 * n, nx), jnp.float32),
                 pltpu.VMEM((8 * n, nx), jnp.float32),
                 pltpu.VMEM((n, 8, nx), jnp.float32),
                 pltpu.VMEM((2, 2, n, nx), jnp.float32),
                 pltpu.VMEM((2, 2, n, nx), jnp.float32),
-                dma((3,)), dma((2,)), dma((3,)), dma((3,)), dma((1,)), dma((1,)), dma((2, 2)), dma((2, 2)),
+                dma((3,)), dma((2,)), dma((4,)), dma((4,)), dma((2,)), dma((1,)), dma((2, 2)), dma((2, 2)),
             ],
             compiler_params=pltpu.CompilerParams(
                 collective_id=0, has_side_effects=True, vmem_limit_bytes=60 * 2**20
             ),
         )(u_field, w_field, temp_field, f32, mats)
-        return jnp.swapaxes(back.reshape(ys, nz, nx), 1, 2)
 
     spec = P(None, "gx", "gz")
     return jax.shard_map(shards, mesh=mesh, in_specs=(spec, spec, spec), out_specs=spec, check_vma=False)

time: 48.8 us -> 48.5 us (level)
    reshape x1 -> x0, local copies, waits for them, and re-layouts: 0.84 us -> none  [shards(): return jnp.swapaxes(back.reshape(ys, nz, nx), 1, 2)]
    unnamed x0 -> x1, local copies, waits for them, and re-layouts: none -> 0.71 us
where the time goes in v6:
time: 48.5 us; the launch traced here: 48.4 us
  Pallas kernels  47.7 us (98%)
  local copies, waits for them, and re-layouts  0.71 us (1%)
    pallas_call x1, Pallas kernels, shards(): pl.pallas_call(functools.partial(kernel, n, layers, cut), out_shape=pltpu...  47.7 us

profile of v6, /device:TPU:1, one launch (start us, length us, event | category | flops | bytes accessed | tf_op | source)
XLA Modules:
  0.0 48.4 jit_solution(17498853486611642994)
XLA Ops:
  0.0 47.7 %shard_map.55 = f32[2,256,128]{2,1,0:T(8,128)S(1)} custom-call(f32[2,256,128]{2,1,0:T(8,128)} %u_hbm.1, f32[2,256,128]{2,1,0:T(8,128)} %w_hbm.1, f32[2,256,128]{2,1,0:T(8,128)} %t_hbm.1, f32[6,256,256]{2,1,0:T(8,128)} %constant.4.clone.f32_hbm, bf16[14,256,256]{2,1,0:T(8,128)(2,1)} %constant.5.clone.mats_hbm), custom_call_target="tpu_custom_call" | custom-call | tf_op jit(solution)/shard_map/pallas_call | solution.py:320
  47.7 0.7 %copy.7 = f32[2,256,128]{2,1,0:T(8,128)} copy(f32[2,256,128]{2,1,0:T(8,128)S(1)} %shard_map.55) | data formatting | bytes 524288

commit v7 on v6

--- a/solution.py
+++ b/solution.py
@@ -136,7 +136,7 @@
 
     def to_peers(src, dst, send_s, recv_s, sign):
         def step(i, carry):
-            p = lax.rem(me + n + sign * i, n)
+            p = lax.rem(me + n + (i if sign > 0 else jnp.where(i % 2 == 1, (i + 1) // 2, -(i // 2))), n)
             pltpu.make_async_remote_copy(
                 src_ref=src(p), dst_ref=dst(me), send_sem=send_s, recv_sem=recv_s,
                 device_id=(p, lay), device_id_type=MESH,

time: 48.5 us -> 48.4 us (level)
  no operation moved by 1% of the time
where the time goes in v7:
time: 48.4 us; the launch traced here: 48.3 us
  Pallas kernels  47.6 us (98%)
  local copies, waits for them, and re-layouts  0.71 us (1%)
    pallas_call x1, Pallas kernels, shards(): pl.pallas_call(functools.partial(kernel, n, layers, cut), out_shape=pltpu...  47.6 us

profile of v7, /device:TPU:1, one launch (start us, length us, event | category | flops | bytes accessed | tf_op | source)
XLA Modules:
  0.0 48.3 jit_solution(5012395291112297781)
XLA Ops:
  0.0 47.6 %shard_map.55 = f32[2,256,128]{2,1,0:T(8,128)S(1)} custom-call(f32[2,256,128]{2,1,0:T(8,128)} %u_hbm.1, f32[2,256,128]{2,1,0:T(8,128)} %w_hbm.1, f32[2,256,128]{2,1,0:T(8,128)} %t_hbm.1, f32[6,256,256]{2,1,0:T(8,128)} %constant.4.clone.f32_hbm, bf16[14,256,256]{2,1,0:T(8,128)(2,1)} %constant.5.clone.mats_hbm), custom_call_target="tpu_custom_call" | custom-call | tf_op jit(solution)/shard_map/pallas_call | solution.py:320
  47.6 0.7 %copy.7 = f32[2,256,128]{2,1,0:T(8,128)} copy(f32[2,256,128]{2,1,0:T(8,128)S(1)} %shard_map.55) | data formatting | bytes 524288

commit v8 on v7

--- a/solution.py
+++ b/solution.py
@@ -110,8 +110,7 @@
         pltpu.make_async_copy(src, fields.at[f], load_sem.at[f])
         for f, src in enumerate((t_hbm, w_hbm, u_hbm))
     ]
-    for c in loads + consts:
-        c.start()
+    loads[0].start()
     nxt_gx = base + lax.rem(b + 1, blocks)
     nxt_gz = lax.rem(lay + jnp.where(b == blocks - 1, 1, 0), layers)
     prv_gx = base + lax.rem(b + blocks - 1, blocks)
@@ -126,6 +125,9 @@
     lax.fori_loop(1, n, greet, 0)
     pl.semaphore_signal(barrier, inc=1, device_id=(nxt_gx, nxt_gz), device_id_type=MESH)
     pl.semaphore_signal(barrier, inc=1, device_id=(prv_gx, prv_gz), device_id_type=MESH)
+
+    for c in loads[1:] + consts:
+        c.start()
 
     def turned(f):
         loads[f].wait()

time: 48.4 us -> 48.4 us (level)
  no operation moved by 1% of the time
where the time goes in v8:
time: 48.4 us; the launch traced here: 48.3 us
  Pallas kernels  47.6 us (98%)
  local copies, waits for them, and re-layouts  0.71 us (1%)
    pallas_call x1, Pallas kernels, shards(): pl.pallas_call(functools.partial(kernel, n, layers, cut), out_shape=pltpu...  47.6 us

profile of v8, /device:TPU:1, one launch (start us, length us, event | category | flops | bytes accessed | tf_op | source)
XLA Modules:
  0.0 48.3 jit_solution(10915031480693188423)
XLA Ops:
  0.0 47.6 %shard_map.55 = f32[2,256,128]{2,1,0:T(8,128)S(1)} custom-call(f32[2,256,128]{2,1,0:T(8,128)} %u_hbm.1, f32[2,256,128]{2,1,0:T(8,128)} %w_hbm.1, f32[2,256,128]{2,1,0:T(8,128)} %t_hbm.1, f32[6,256,256]{2,1,0:T(8,128)} %constant.4.clone.f32_hbm, bf16[14,256,256]{2,1,0:T(8,128)(2,1)} %constant.5.clone.mats_hbm), custom_call_target="tpu_custom_call" | custom-call | tf_op jit(solution)/shard_map/pallas_call | solution.py:322
  47.6 0.7 %copy.7 = f32[2,256,128]{2,1,0:T(8,128)} copy(f32[2,256,128]{2,1,0:T(8,128)S(1)} %shard_map.55) | data formatting | bytes 524288
